TPU v7x, 32 devices: a whole 2x2x4 slice. The times are simulated.
32 devices in a mesh: prompt: 4 (over z), decode: 8 (over y, x, core).
Axes of the slice: x: 2, y: 2, z: 4, core: 2. Of those that a mesh axis runs over, the one named last changes fastest.
Arguments:
- hidden_in: bfloat16 [16, 32, 4096], P('prompt', 'decode'), may hold values from -6 to 6
- queries: bfloat16 [16, 32, 4096], P('prompt', 'decode'), may hold values from -8 to 8
- new_kv: bfloat16 [16, 32, 512], P('prompt', 'decode'), may hold values from -8 to 8
- prompt_kv: bfloat16 [16, 4096, 512], P('prompt', 'decode'), may hold values from -8 to 8
- sample_kv: bfloat16 [16, 32, 64, 512], P('prompt', 'decode'), may hold values from -8 to 8
- counts: int32 [16, 32], P('prompt', 'decode'), may hold values from 1 to 64, 1024 in all within a row
- out_proj: bfloat16 [4096, 4096], P('decode'), may hold values from -0.5 to 0.5
- norm_gain: float32 [4096], replicated, may hold values from 0.5 to 1.5
- expert_ids: int32 [4, 8, 16, 8], P('prompt', 'decode'), may hold values from 0 to 31, all different within a row; in each aligned block of 16 rows (0 to 15, 16 to 31, ..., all dimensions but the last counted through in order) at most 8 rows name the same one
- expert_gates: float32 [4, 8, 16, 8], P('prompt', 'decode'), may hold values from 0.05 to 0.35
- w_gate: bfloat16 [32, 4096, 768], P(('prompt', 'decode')), may hold values from -0.09375 to 0.09375
- w_up: bfloat16 [32, 4096, 768], P(('prompt', 'decode')), may hold values from -0.09375 to 0.09375
- w_down: bfloat16 [32, 768, 4096], P(('prompt', 'decode')), may hold values from -0.21875 to 0.21875
Outputs:
- mixed: bfloat16 [16, 32, 4096], P('prompt', 'decode')
Inputs may be any that keep to these rules, and one draw needn't show every extreme that they name: `expert_ids`: each row names 8 different experts; among the 16 rows of one [a, b] block no expert is named more than 8 times, and in some block some expert exactly 8 times. `counts`: for every prompt the largest count is 64.
All inputs are finite; a program needn't handle non-finite values. No bound on the sum of `counts` on one device may be relied on, other than what follows from the above.
Results may differ from a plain program's by a relative error of at most 0.0073.
Values may be sent and summed in bfloat16 or wider, within the bound.
A program may use at most 128 MiB of HBM per device.

v0:
```python
import jax
import jax.numpy as jnp
from jax import lax
from jax.sharding import PartitionSpec as P

H = 32
KVH = 2
HD = 128
TOPK = 8


very_low = -1e30


def split_pages(page_rows, kv_heads, head_width):
    keys_part = page_rows[..., : kv_heads * head_width]
    values_part = page_rows[..., kv_heads * head_width :]
    shape_out = page_rows.shape[:-1] + (kv_heads, head_width)
    return (keys_part.reshape(shape_out), values_part.reshape(shape_out))


def block_partials(grouped, page_rows, blocks, score_scale):
    kv_heads, head_width = (grouped.shape[3], grouped.shape[5])
    prompts, length = (page_rows.shape[0], page_rows.shape[1])
    keys_part, values_part = split_pages(
        page_rows.reshape(prompts, blocks, length // blocks, page_rows.shape[2]),
        kv_heads,
        head_width,
    )
    scores = (
        jnp.einsum("npskgd,pcbkd->cnpskgb", grouped, keys_part, preferred_element_type=jnp.float32)
        * score_scale
    )
    maxima = jnp.max(scores, axis=-1)
    weights = jnp.exp(scores - maxima[..., None])
    totals = jnp.sum(weights, axis=-1)
    blended = jnp.einsum(
        "cnpskgb,pcbkd->cnpskgd",
        weights.astype(jnp.bfloat16),
        values_part,
        preferred_element_type=jnp.float32,
    )
    return ((blended / totals[..., None]).astype(jnp.bfloat16), maxima, totals)


def sample_partials(grouped, fresh_rows, cache_rows, lengths, score_scale):
    kv_heads, head_width = (grouped.shape[1], grouped.shape[3])
    cache_keys, cache_values = split_pages(cache_rows, kv_heads, head_width)
    fresh_key, fresh_value = split_pages(fresh_rows, kv_heads, head_width)
    scores = (
        jnp.einsum("rkgd,rtkd->rkgt", grouped, cache_keys, preferred_element_type=jnp.float32)
        * score_scale
    )
    fresh_score = (
        jnp.einsum("rkgd,rkd->rkg", grouped, fresh_key, preferred_element_type=jnp.float32)
        * score_scale
    )
    keep_mask = (jnp.arange(cache_rows.shape[1], dtype=jnp.int32)[None, :] < lengths[:, None])[
        :, None, None, :
    ]
    masked = jnp.where(keep_mask, scores, very_low)
    maxima = jnp.maximum(jnp.max(masked, axis=-1), fresh_score)
    weights = jnp.exp(masked - maxima[..., None])
    fresh_weight = jnp.exp(fresh_score - maxima)
    totals = jnp.sum(weights, axis=-1) + fresh_weight
    fresh_rounded = lax.optimization_barrier(fresh_weight.astype(jnp.bfloat16)).astype(jnp.float32)
    blended = jnp.einsum(
        "rkgt,rtkd->rkgd",
        weights.astype(jnp.bfloat16),
        cache_values,
        preferred_element_type=jnp.float32,
    )
    blended = blended + fresh_rounded[..., None] * fresh_value.astype(jnp.float32)[:, :, None, :]
    return ((blended / totals[..., None]).astype(jnp.bfloat16), maxima, totals)


def merge_blocks(outputs, maxima, totals):
    best = jnp.max(maxima, axis=0)
    factors = jnp.exp(maxima - best[None]) * totals
    joined = (
        jnp.sum(factors[..., None] * outputs.astype(jnp.float32), axis=0)
        / jnp.sum(factors, axis=0)[..., None]
    )
    return joined.astype(jnp.bfloat16).reshape(joined.shape[0], joined.shape[1] * joined.shape[2])


def expert_ffn(rows_in, gate_matrix, up_matrix, down_matrix):
    gated = jnp.dot(rows_in, gate_matrix, preferred_element_type=jnp.float32)
    lifted = jnp.dot(rows_in, up_matrix, preferred_element_type=jnp.float32)
    hidden_act = (jax.nn.silu(gated) * lifted).astype(jnp.bfloat16)
    return jnp.dot(hidden_act, down_matrix, preferred_element_type=jnp.float32).astype(jnp.bfloat16)


def per_device(
    hidden_in,
    queries,
    new_kv,
    prompt_kv,
    sample_kv,
    counts,
    out_proj,
    norm_gain,
    expert_ids,
    expert_gates,
    w_gate,
    w_up,
    w_down,
):
    prompts, samples, model_width = hidden_in.shape
    row_total = prompts * samples
    groups = H // KVH
    score_scale = HD ** (-0.5)
    splits = lax.axis_size("decode")
    grouped = queries.reshape(prompts, samples, KVH, groups, HD)
    local_out, local_max, local_sum = sample_partials(
        grouped.reshape(row_total, KVH, groups, HD),
        new_kv.reshape(row_total, new_kv.shape[-1]),
        sample_kv.reshape(row_total, sample_kv.shape[2], sample_kv.shape[3]),
        counts.reshape(row_total),
        score_scale,
    )
    page_all = lax.all_gather(prompt_kv, "decode", axis=1, tiled=True)
    remote_out, remote_max, remote_sum = block_partials(
        grouped[None], page_all, splits, score_scale
    )
    outputs = jnp.concatenate(
        [remote_out.reshape(splits, row_total, H, HD), local_out.reshape(1, row_total, H, HD)],
        axis=0,
    )
    maxima = jnp.concatenate(
        [remote_max.reshape(splits, row_total, H), local_max.reshape(1, row_total, H)], axis=0
    )
    totals = jnp.concatenate(
        [remote_sum.reshape(splits, row_total, H), local_sum.reshape(1, row_total, H)], axis=0
    )
    attention_rows = merge_blocks(outputs, maxima, totals)
    attention = lax.all_to_all(attention_rows, "decode", split_axis=1, concat_axis=0, tiled=True)
    projected = lax.psum_scatter(
        jnp.dot(attention, out_proj, preferred_element_type=jnp.float32),
        "decode",
        scatter_dimension=0,
        tiled=True,
    )
    residual_sum = hidden_in.reshape(row_total, model_width).astype(jnp.float32) + projected
    normed = (
        residual_sum
        * lax.rsqrt(jnp.mean(residual_sum * residual_sum, axis=-1, keepdims=True) + 1e-06)
        * norm_gain
    ).astype(jnp.bfloat16)
    prompt_size = lax.axis_size("prompt")
    experts = prompt_size * splits
    capacity = max(2, 2 * row_total * TOPK // experts)
    chosen = expert_ids.reshape(row_total * TOPK)
    onehot_table = (chosen[:, None] == jnp.arange(experts, dtype=jnp.int32)[None, :]).astype(
        jnp.int32
    )
    earlier = jnp.cumsum(onehot_table, axis=0) - onehot_table
    ranking = jnp.sum(earlier * onehot_table, axis=1)
    slot_index = chosen * capacity + ranking
    placement = jnp.any(
        slot_index.reshape(row_total, TOPK)[:, :, None]
        == jnp.arange(experts * capacity, dtype=jnp.int32)[None, None, :],
        axis=1,
    )
    outgoing = jnp.einsum(
        "re,rd->ed", placement.astype(jnp.bfloat16), normed, preferred_element_type=jnp.float32
    ).astype(jnp.bfloat16)
    expert_block = lax.all_to_all(
        outgoing.reshape(experts, capacity, model_width),
        ("prompt", "decode"),
        split_axis=0,
        concat_axis=0,
        tiled=True,
    )
    sources = expert_block.shape[0]
    slots_here = expert_block.shape[1]
    finished = expert_ffn(
        expert_block.reshape(sources * slots_here, model_width), w_gate[0], w_up[0], w_down[0]
    )
    returned = lax.all_to_all(
        finished.reshape(sources, slots_here, model_width),
        ("prompt", "decode"),
        split_axis=0,
        concat_axis=0,
        tiled=True,
    )
    gathered_rows = returned.reshape(experts * capacity, model_width)[slot_index]
    blended = jnp.sum(
        expert_gates.reshape(row_total, TOPK, 1)
        * gathered_rows.reshape(row_total, TOPK, model_width).astype(jnp.float32),
        axis=1,
    )
    return (residual_sum + blended).astype(jnp.bfloat16).reshape(prompts, samples, model_width)


def solution(mesh):
    in_specs = (
        P("prompt", "decode", None),
        P("prompt", "decode", None),
        P("prompt", "decode", None),
        P("prompt", "decode", None),
        P("prompt", "decode", None, None),
        P("prompt", "decode"),
        P("decode", None),
        P(),
        P("prompt", "decode", None, None),
        P("prompt", "decode", None, None),
        P(("prompt", "decode"), None, None),
        P(("prompt", "decode"), None, None),
        P(("prompt", "decode"), None, None),
    )
    out_specs = P("prompt", "decode", None)
    return jax.shard_map(
        per_device, mesh=mesh, in_specs=in_specs, out_specs=out_specs, check_vma=False
    )
```

profile of v0, /device:TPU:0, one launch (start us, length us, event | category | flops | bytes accessed | tf_op | source)
XLA Modules:
  0.0 339.6 jit_solution(11517964896636362579)
XLA Ops:
  6.5 0.7 all-gather.2.cloned.1.call-update
  7.3 1.1 reshape_reshape.3
  8.4 1.1 reshape.225
  9.4 0.8 lt.33
  10.2 0.7 reshape.228
  11.0 0.2 fusion.71
  11.2 1.4 slice_bitcast_fusion.1
  12.6 0.5 fusion.70
  13.1 0.1 reshape.230
  13.2 0.1 concatenate.26
  13.3 0.3 fusion.53
  13.6 0.1 concatenate.29
  13.7 0.3 fusion.42
  14.0 87.8 %all-gather.2.cloned.1.call-done = bf16[4,4096,512]{2,1,0:T(8,128)(2,1)} async-done(((bf16[4,512,512]{2,1,0:T(8,128)(2,1)}), bf16[4,4096,512]{2,1,0:T(8,128)(2,1)}) %all-gather.2.cloned.1.call-update) | async-done | bytes 16777232 | tf_op jit(solution)/shard_map/all_gather | solution.py:122
  101.9 11.5 %fusion.69 = (bf16[4,8,512,256]{3,2,1,0:T(8,128)(2,1)}, bf16[4,8,512,256]{3,2,1,0:T(8,128)(2,1)}) fusion(bf16[4,8,512,512]{3,2,1,0:T(8,128)(2,1)} %bitcast.114), kind=kLoop, calls=%fused_computation.78 | loop fusion | bytes 33554432 | tf_op jit(solution)/shard_map/slice | solution.py:16
  113.3 11.4 %copy.89 = bf16[4,8,512,256]{2,3,1,0:T(8,128)(2,1)} copy(bf16[4,8,512,256]{3,2,1,0:T(8,128)(2,1)} %get-tuple-element.11) | data formatting | bytes 16777216 | tf_op jit(solution)/shard_map/slice | solution.py:16
  124.7 4.7 %bitcast_reduce_fusion.1 = (f32[8,4,4,2,16]{4,2,0,3,1:T(4,128)S(1)}, f32[4,2,8,512,4,16]{3,5,4,2,1,0:T(8,128)S(1)}) fusion(bf16[4,8,512,2,128,1]{2,4,3,1,0,5:T(8,128)(2,1)} %bitcast.112, bf16[4,4,2,16,128]{4,3,2,1,0:T(8,128)(2,1)S(1)} %reshape.225), kind=kOutput, calls=%fused_computation.5 | convolution fusion | flops 541061120 | bytes 16924672 | tf_op jit(solution)/shard_map/npskgd,pcbkd->cnpskgb/dot_general | solution.py:31
  129.4 0.1 copy.92
  129.5 4.1 %bitcast_reduce_fusion = (f32[4,4,2,16]{3,1,2,0:T(4,128)S(1)}, f32[8,4,4,2,16]{4,2,0,3,1:T(4,128)S(1)}, bf16[8,4,4,2,16,512]{5,4,2,0,3,1:T(8,128)(2,1)}) fusion(f32[4,2,8,512,4,16]{3,5,4,2,1,0:T(8,128)S(1)} %get-tuple-element.23, f32[8,4,4,2,16]{4,2,0,3,1:T(4,128)S(1)} %get-tuple-element.22), kind=kLoop, calls=%fused_computation.4 | loop fusion | flops 10481152 | bytes 12617728 | tf_op jit(solution)/shard_map/reduce_max | solution.py:78
  133.6 0.1 concatenate.25
  133.8 0.1 reduce_max.38
  133.9 0.1 copy.95
  134.0 0.1 concatenate.28
  134.1 11.4 %copy.96 = bf16[4,8,512,256]{2,3,1,0:T(8,128)(2,1)} copy(bf16[4,8,512,256]{3,2,1,0:T(8,128)(2,1)} %get-tuple-element.12) | data formatting | bytes 16777216 | tf_op jit(solution)/shard_map/slice | solution.py:17
  145.4 7.7 %fusion.23 = bf16[8,1,4,4,2,16,128]{6,5,3,4,2,0,1:T(8,128)(2,1)S(1)} fusion(bf16[4,8,512,2,128,1]{2,4,3,1,0,5:T(8,128)(2,1)} %bitcast.115, bf16[8,4,4,2,16,512]{5,4,2,0,3,1:T(8,128)(2,1)} %get-tuple-element.13, f32[8,4,4,2,16]{4,2,0,3,1:T(4,128)S(1)} %get-tuple-element.6), kind=kOutput, calls=%fused_computation.27 | convolution fusion | flops 537919488 | bytes 13647872 | tf_op jit(solution)/shard_map/cnpskgb,pcbkd->cnpskgd/dot_general | solution.py:37
  153.1 0.2 copy.100
  153.4 0.8 multiply_reduce_fusion
  154.2 0.1 divide_convert_fusion
  154.3 0.1 convert_element_type.82
  154.5 8.1 %all_to_all.26 = bf16[16,8,512]{2,0,1:T(8,128)(2,1)S(1)} all-to-all(bf16[16,8,512]{2,0,1:T(8,128)(2,1)S(1)} %copy.102), channel_id=1, replica_groups=mesh['prompt'=4,'decode'=8] {'decode'}, dimensions={1} | all-to-all | bytes 262144 | tf_op jit(solution)/shard_map/all_to_all | solution.py:137
  162.5 4.3 %fusion.72 = f32[128,4096]{1,0:T(8,128)} fusion(bf16[128,512]{1,0:T(8,128)(2,1)S(1)} %bitcast.118, bf16[512,4096]{1,0:T(8,128)(2,1)} %param.19), kind=kOutput, calls=%fused_computation.81 | convolution fusion | flops 536870912 | bytes 6422528 | tf_op jit(solution)/shard_map/dot_general | solution.py:139
  167.0 0.1 eq.28
  167.1 0.1 fusion.62
  167.2 0.2 reduce_window_sum.11
  167.4 0.2 select_reduce_fusion
  167.8 0.1 fusion.59
  167.9 39.4 %reduce-scatter.2.cloned.1.call-done = f32[16,4096]{1,0:T(8,128)} async-done(((f32[128,4096]{1,0:T(8,128)}), f32[16,4096]{1,0:T(8,128)}) %reduce-scatter.2.cloned.1.call-update) | async-done | bytes 262160 | tf_op jit(solution)/shard_map/reduce_scatter | solution.py:138
  207.4 1.1 multiply_reduce_fusion.1
  208.5 0.7 fusion.19
  209.3 53.1 %all_to_all.27 = bf16[32,8,4096]{2,1,0:T(8,128)(2,1)S(1)} all-to-all(bf16[32,8,4096]{2,1,0:T(8,128)(2,1)S(1)} %fusion.19), channel_id=1, replica_groups=mesh['prompt'=4,'decode'=8] {'prompt','decode'}, dimensions={0} | all-to-all | bytes 4194304 | tf_op jit(solution)/shard_map/all_to_all | solution.py:168
  262.4 4.6 %fusion.11 = f32[256,768]{1,0:T(8,128)S(1)} fusion(bf16[1,4096,768]{2,1,0:T(8,128)(2,1)} %param.23, bf16[32,8,4096]{2,1,0:T(8,128)(2,1)S(1)} %all_to_all.27), kind=kOutput, calls=%fused_computation.15 | convolution fusion | flops 1610612736 | bytes 9175040 | tf_op jit(solution)/shard_map/dot_general | solution.py:88
  266.9 10.5 %fusion.16 = bf16[32,8,4096]{2,1,0:T(8,128)(2,1)} fusion(bf16[1,768,4096]{2,1,0:T(8,128)(2,1)} %param.25, bf16[1,4096,768]{2,1,0:T(8,128)(2,1)} %param.24, bf16[32,8,4096]{2,1,0:T(8,128)(2,1)S(1)} %all_to_all.27, f32[256,768]{1,0:T(8,128)S(1)} %fusion.11), kind=kOutput, calls=%fused_computation.19 | convolution fusion | flops 3223453696 | bytes 17563648 | tf_op jit(solution)/shard_map/dot_general | solution.py:91
  277.5 3.7 %all-to-all-start.2 = ((bf16[32,8,4096]{2,1,0:T(8,128)(2,1)}), bf16[32,8,4096]{2,1,0:T(8,128)(2,1)S(1)}, u32[]{:S(2)}, u32[]{:S(2)}) async-start(bf16[32,8,4096]{2,1,0:T(8,128)(2,1)} %fusion.16), calls=%async_computation.3 | async-start | bytes 4194304 | tf_op jit(solution)/shard_map/all_to_all | solution.py:180
  281.2 0.1 mul.141
  281.4 48.6 %all-to-all-done.2 = bf16[32,8,4096]{2,1,0:T(8,128)(2,1)S(1)} async-done(((bf16[32,8,4096]{2,1,0:T(8,128)(2,1)}), bf16[32,8,4096]{2,1,0:T(8,128)(2,1)S(1)}, u32[]{:S(2)}, u32[]{:S(2)}) %all-to-all-start.2) | async-done | bytes 2097184 | tf_op jit(solution)/shard_map/all_to_all | solution.py:180
  330.0 1.2 gather_fusion
  331.2 0.8 fusion.22
  332.1 0.7 reshape.240
  (35 shorter events, 0.9 us)
Async XLA Ops:
  6.5 95.3 %all-gather.2.cloned.1.call-start = ((), (), s32[]{:S(2)}) async-start(), calls=%async_computation.4 | async-start | bytes 18874368 | tf_op jit(solution)/shard_map/all_gather | solution.py:122
  7.3 200.1 %reduce-scatter.2.cloned.1.call-start = ((), (), s32[]{:S(2)}) async-start(), calls=%async_computation.5 | async-start | bytes 2359296 | tf_op jit(solution)/shard_map/reduce_scatter | solution.py:138
  162.5 4.4 %copy-start.1 = (s32[1,1,16,8]{2,3,1,0:T(8,128)S(1)}, s32[1,1,16,8]{2,3,1,0:T(8,128)}, u32[]{:S(2)}) copy-start(s32[1,1,16,8]{2,3,1,0:T(8,128)} %param.21) | copy-start | bytes 1540
  162.5 5.2 %copy-start = (bf16[4,4,4096]{2,1,0:T(4,128)(2,1)S(1)}, bf16[4,4,4096]{2,1,0:T(4,128)(2,1)}, u32[]{:S(2)}) copy-start(bf16[4,4,4096]{2,1,0:T(4,128)(2,1)} %param.13) | copy-start | bytes 393220
  162.5 45.9 %copy-start.2 = (f32[4096]{0:T(1024)S(1)}, f32[4096]{0:T(1024)}, u32[]{:S(2)}) copy-start(f32[4096]{0:T(1024)} %param.20) | copy-start | bytes 49156
  277.5 3.9 %copy-start.3 = (f32[1,1,16,8]{2,3,1,0:T(8,128)S(1)}, f32[1,1,16,8]{2,3,1,0:T(8,128)}, u32[]{:S(2)}) copy-start(f32[1,1,16,8]{2,3,1,0:T(8,128)} %param.22) | copy-start | bytes 1540
  277.5 52.6 %all-to-all-start.2 = ((bf16[32,8,4096]{2,1,0:T(8,128)(2,1)}), bf16[32,8,4096]{2,1,0:T(8,128)(2,1)S(1)}, u32[]{:S(2)}, u32[]{:S(2)}) async-start(bf16[32,8,4096]{2,1,0:T(8,128)(2,1)} %fusion.16), calls=%async_computation.3 | async-start | bytes 4194304 | tf_op jit(solution)/shard_map/all_to_all | solution.py:180
Sparse Core Ops, SparseCore 0:
  9.3 92.5 all-gather.1
  167.0 40.2 reduce-scatter.1
where the time goes:
time: 341 us; the launch traced here: 340 us
  waiting for transfers between devices  177 us (52%)
  blocking collectives  61.2 us (18%)
  local copies, waits for them, and re-layouts  42.9 us (13%)
  matrix products  33.5 us (10%)
  between operations  13.6 us (4%)
  other arithmetic  8 us (2%)
  starting transfers between devices  3.71 us (1%)
    all_gather x1, waiting for transfers between devices, per_device(): page_all = lax.all_gather(prompt_kv, 'decode', axis=1, tiled=True)  87.8 us
    all_to_all x1, blocking collectives, per_device(): lax.all_to_all(outgoing.reshape(experts, capacity, model_width), ('prompt...  53.1 us
    all_to_all x1, waiting for transfers between devices, per_device(): lax.all_to_all(finished.reshape(sources, slots_here, model_width), ('prom...  48.6 us
    reduce_scatter x1, waiting for transfers between devices, per_device(): lax.psum_scatter(jnp.dot(attention, out_proj, preferred_element_type=jnp....  39.4 us
    slice x2, local copies, waits for them, and re-layouts, split_pages(): keys_part = page_rows[..., :kv_heads * head_width]  22.8 us
    slice x1, local copies, waits for them, and re-layouts, split_pages(): values_part = page_rows[..., kv_heads * head_width:]  11.4 us
    dot_general x1, matrix products, expert_ffn(): jnp.dot(hidden_act, down_matrix, preferred_element_type=jnp.float32)  10.5 us
    all_to_all x1, blocking collectives, per_device(): lax.all_to_all(attention_rows, 'decode', split_axis=1, concat_axis=0, til...  8.07 us
  transfers between devices with their start and end apart: 3, of which 3 were waited for; matrix products, arithmetic and copies ran while one was open for 2% of the time, Pallas kernels for 0%

commit v1 on v0

v1 whole, which is shorter than its diff:
```python
import functools

import jax
import jax.numpy as jnp
from jax import lax
from jax.experimental import pallas as pl
from jax.experimental.pallas import tpu as pltpu
from jax.sharding import PartitionSpec as P

H = 32
KVH = 2
HD = 128
TOPK = 8
GROUPS = H // KVH
SCALE = HD ** (-0.5)
LOW = -1e30
MESH = pl.DeviceIdType.MESH
BF = jnp.bfloat16
F32 = jnp.float32


def nbits(n):
    return n.bit_length() - 1


def bit_of(axis, k):
    return lax.rem(lax.axis_index(axis) // (1 << k), 2)


def partner(axis, k):
    me = lax.axis_index(axis)
    return {axis: me + (1 - 2 * bit_of(axis, k)) * (1 << k)}


def cube_index(dims, fixed, flip=None):
    out = []
    for dim in dims:
        if dim == flip:
            out.append(1 - bit_of(*dim))
        elif dim in fixed:
            out.append(bit_of(*dim))
        else:
            out.append(slice(None))
    return tuple(out)


def gather_copy(ref, dims, order, step, tail, ssem, rsem):
    fixed = set(order[step:])
    view = ref.at[cube_index(dims, fixed) + tail]
    return pltpu.make_async_remote_copy(
        src_ref=view, dst_ref=view, send_sem=ssem, recv_sem=rsem,
        device_id=partner(*order[step]), device_id_type=MESH,
    )


def scatter_copy(ref, land, dims, order, step, tail, ssem, rsem):
    fixed = set(order[:step])
    view = ref.at[cube_index(dims, fixed, flip=order[step]) + tail]
    return pltpu.make_async_remote_copy(
        src_ref=view, dst_ref=land, send_sem=ssem, recv_sem=rsem,
        device_id=partner(*order[step]), device_id_type=MESH,
    )


def attention_kernel(
    nd, hpd, tdt,
    q_ref, kv_ref, skv_ref, nkv_ref, bias_ref, wo_ref, hid_ref, gain_ref, gates_ref,
    res_ref, pay_ref,
    qall, kv, skv, wo, obuf, orecv, stat, strecv, acc, *rest,
):
    nb = nbits(nd)
    lands = [rest[:nb], rest[nb : 2 * nb]]
    local_sem, q_s, q_r, o_s, o_r, t_s, t_r, p_s, p_r = rest[2 * nb :]
    me = lax.axis_index("decode")
    dims = [("decode", k) for k in range(nb - 1, -1, -1)]
    orders = [dims[:-1][::-1] + dims[-1:], dims[:-1] + dims[-1:]]
    tile = hpd * 4
    kv_heads_dev = GROUPS // hpd

    loads = [
        pltpu.make_async_copy(skv_ref, skv, local_sem.at[0]),
        pltpu.make_async_copy(kv_ref, kv, local_sem.at[1]),
        pltpu.make_async_copy(wo_ref, wo, local_sem.at[2]),
    ]
    for load in loads:
        load.start()

    barrier = pltpu.get_barrier_semaphore()
    for k in range(1, nd):
        pl.semaphore_signal(
            barrier, inc=1, device_id={"decode": lax.rem(me + k, nd)}, device_id_type=MESH
        )
    mine = cube_index(dims, set(dims))
    for part in range(2):
        qall[(part,) + mine] = q_ref[2 * part : 2 * part + 2]
    pl.semaphore_wait(barrier, nd - 1)

    def q_copy(part, step):
        return gather_copy(
            qall.at[part], dims, orders[part], step, (), q_s.at[part, step], q_r.at[part, step]
        )

    for part in range(2):
        q_copy(part, 0).start()

    loads[0].wait()
    for g in range(KVH):
        ks, vs = slice(g * HD, (g + 1) * HD), slice((KVH + g) * HD, (KVH + g + 1) * HD)
        pad = jnp.zeros((112, HD), BF)
        keys = jnp.concatenate([skv[:, ks], nkv_ref[:, ks], pad], axis=0)
        values = jnp.concatenate([skv[:, vs], nkv_ref[:, vs], pad], axis=0)
        rows = q_ref[:, g * kv_heads_dev : (g + 1) * kv_heads_dev].astype(BF)
        rows = rows.reshape(4 * kv_heads_dev * tile, HD)
        scores = lax.dot_general(
            rows, keys, (((1,), (1,)), ((), ())), preferred_element_type=F32
        ) * SCALE
        cols = scores.shape[1]
        bias = bias_ref[...].reshape(4, 1, tile, cols)
        masked = jnp.where(bias < 0, LOW, scores.reshape(4, kv_heads_dev, tile, cols))
        masked = masked.reshape(scores.shape)
        top = jnp.max(masked, axis=1, keepdims=True)
        weights = jnp.exp(masked - top)
        total = jnp.sum(weights, axis=1, keepdims=True)
        out = jnp.dot(weights.astype(BF), values, preferred_element_type=F32) / total
        out = out.astype(tdt).reshape(4, kv_heads_dev, tile, HD)
        lane = lax.broadcasted_iota(jnp.int32, (rows.shape[0], HD), 1)
        st = jnp.where(lane == 0, top, jnp.where(lane == 1, total, 0.0))
        st = st.reshape(4, kv_heads_dev, tile, HD)
        for hq in range(kv_heads_dev):
            j = g * kv_heads_dev + hq
            obuf[j, :, nd] = out[:, hq]
            block = st[:, hq].reshape(4 * tile, HD)
            block = jnp.concatenate([block, jnp.zeros((HD - 4 * tile, HD), F32)], axis=0)
            stat[j, 8:16] = block.T[0:8]

    for step in range(nb):
        for part in range(2):
            q_copy(part, step).wait()
            if step + 1 < nb:
                q_copy(part, step + 1).start()

    def peer_copies(j):
        return (
            pltpu.make_async_remote_copy(
                src_ref=obuf.at[j], dst_ref=orecv.at[me], send_sem=o_s.at[j], recv_sem=o_r.at[me],
                device_id={"decode": j}, device_id_type=MESH),
            pltpu.make_async_remote_copy(
                src_ref=stat.at[j], dst_ref=strecv.at[me], send_sem=t_s.at[j], recv_sem=t_r.at[me],
                device_id={"decode": j}, device_id_type=MESH),
        )

    def from_peer(j):
        return (
            pltpu.make_async_remote_copy(
                src_ref=obuf.at[j], dst_ref=orecv.at[j], send_sem=o_s.at[j], recv_sem=o_r.at[j],
                device_id={"decode": j}, device_id_type=MESH),
            pltpu.make_async_remote_copy(
                src_ref=stat.at[j], dst_ref=strecv.at[j], send_sem=t_s.at[j], recv_sem=t_r.at[j],
                device_id={"decode": j}, device_id_type=MESH),
        )

    loads[1].wait()
    m_rows = nd * kv_heads_dev * tile
    for g in range(KVH):
        lane = lax.broadcasted_iota(jnp.int32, (m_rows, HD), 1)
        st = jnp.zeros((m_rows, HD), F32)
        for p in range(4):
            keys = kv[p, :, g * HD : (g + 1) * HD]
            values = kv[p, :, (KVH + g) * HD : (KVH + g + 1) * HD]
            q_at = (p // 2,) + (slice(None),) * nb + (p % 2, slice(g * kv_heads_dev, (g + 1) * kv_heads_dev))
            rows = qall[q_at].astype(BF).reshape(m_rows, HD)
            scores = lax.dot_general(
                rows, keys, (((1,), (1,)), ((), ())), preferred_element_type=F32
            ) * SCALE
            top = jnp.max(scores, axis=1, keepdims=True)
            weights = jnp.exp(scores - top)
            total = jnp.sum(weights, axis=1, keepdims=True)
            out = jnp.dot(weights.astype(BF), values, preferred_element_type=F32) / total
            out = out.astype(tdt).reshape(nd, kv_heads_dev, tile, HD)
            for hq in range(kv_heads_dev):
                obuf[g * kv_heads_dev + hq, p, 0:nd] = out[:, hq]
            st = jnp.where(lane == 2 * p, top, jnp.where(lane == 2 * p + 1, total, st))
        st = st.reshape(nd, kv_heads_dev, tile, HD)
        for hq in range(kv_heads_dev):
            stat[g * kv_heads_dev + hq, 0:8] = st[:, hq].reshape(nd * tile, HD).T[0:8]
        for hq in range(kv_heads_dev):
            j = g * kv_heads_dev + hq

            @pl.when(j != me)
            def _():
                for copy in peer_copies(j):
                    copy.start()

            @pl.when(j == me)
            def _():
                orecv[me] = obuf[me]
                strecv[me] = stat[me]

    for j in range(nd):

        @pl.when(j != me)
        def _():
            for copy in from_peer(j):
                copy.wait()

    turned = strecv[...].reshape(nd * 16, HD).T
    merged = []
    for p in range(4):
        tops = [turned[:, b * 16 + 2 * p : b * 16 + 2 * p + 1] for b in range(nd)]
        sums = [turned[:, b * 16 + 2 * p + 1 : b * 16 + 2 * p + 2] for b in range(nd)]
        span = slice(p * tile, (p + 1) * tile)
        tops.append(jnp.concatenate([turned[span, d * 16 + 8 : d * 16 + 9] for d in range(nd)], axis=0))
        sums.append(jnp.concatenate([turned[span, d * 16 + 9 : d * 16 + 10] for d in range(nd)], axis=0))
        best = functools.reduce(jnp.maximum, tops)
        whole = jnp.zeros_like(best)
        joined = jnp.zeros((nd * tile, HD), F32)
        for b in range(nd + 1):
            factor = jnp.exp(tops[b] - best) * sums[b]
            if b < nd:
                piece = orecv[b, p, 0:nd].reshape(nd * tile, HD)
            else:
                piece = jnp.concatenate([orecv[d, p, nd] for d in range(nd)], axis=0)
            whole = whole + factor
            joined = joined + factor * piece.astype(F32)
        merged.append((joined / whole).astype(BF))
    merged = jnp.concatenate(merged, axis=0)
    row = lax.broadcasted_iota(jnp.int32, (nd * 16, 4 * nd * tile), 0)
    col = lax.broadcasted_iota(jnp.int32, (nd * 16, 4 * nd * tile), 1)
    at = (row // 4) % 4 * (nd * tile) + row // 16 * tile + row % 4
    picked = []
    for h in range(hpd):
        select = jnp.where(col == at + h * 4, 1.0, 0.0).astype(BF)
        picked.append(jnp.dot(select, merged, preferred_element_type=F32).astype(BF))
    attention = jnp.concatenate(picked, axis=1)

    loads[2].wait()
    width = wo.shape[1]
    half = width // 2
    cube = (2,) * nb
    for c in range(0, width, 512):
        part_sum = jnp.dot(attention, wo[:, c : c + 512], preferred_element_type=F32)
        acc[(slice(None),) * (nb + 1) + (slice(c, c + 512),)] = part_sum.astype(BF).reshape(cube + (16, 512))
    s_orders = [dims[-1:] + dims[:-1][::-1], dims[-1:] + dims[:-1]]

    def p_copy(part, step):
        tail = (slice(None), slice(part * half, (part + 1) * half))
        return scatter_copy(
            acc, lands[part][step], dims, s_orders[part], step, tail,
            p_s.at[part, step], p_r.at[part, step],
        )

    for part in range(2):
        p_copy(part, 0).start()
    for step in range(nb):
        for part in range(2):
            p_copy(part, step).wait()
            span = slice(part * half, (part + 1) * half)
            at = cube_index(dims, set(s_orders[part][: step + 1])) + (slice(None), span)
            summed = acc[at].astype(F32) + lands[part][step][...].astype(F32)
            if step + 1 < nb:
                acc[at] = summed.astype(BF)
                p_copy(part, step + 1).start()
            else:
                res_ref[:, span] = hid_ref[:, span].astype(F32) + summed
    residual = res_ref[...]
    scale = lax.rsqrt(jnp.mean(residual * residual, axis=1, keepdims=True) + 1e-06)
    pay_ref[:, 0:width] = (residual * scale * gain_ref[...]).astype(BF)
    pay_ref[:, width:] = gates_ref[...]


def expert_kernel(
    np_, nd, lead, pay_ref, res_ref, wg_ref, wu_ref, wd_ref, out_ref, xbuf, wg, wu, wd, *rest
):
    bp, bd = nbits(np_), nbits(nd)
    nb = bp + bd
    lands = [rest[:nb], rest[nb : 2 * nb]]
    local_sem, g_s, g_r, p_s, p_r = rest[2 * nb :]
    prompt = [("prompt", k) for k in range(bp - 1, -1, -1)]
    decode = [("decode", k) for k in range(bd - 1, -1, -1)]
    dims = prompt + decode
    orders = [prompt + decode, prompt + decode[:-1][::-1] + decode[-1:]]
    width = res_ref.shape[1]
    full = pay_ref.shape[1]
    loads = [
        pltpu.make_async_copy(wg_ref, wg, local_sem.at[0]),
        pltpu.make_async_copy(wu_ref, wu, local_sem.at[1]),
        pltpu.make_async_copy(wd_ref, wd, local_sem.at[2]),
    ]
    for load in loads:
        load.start()
    barrier = pltpu.get_barrier_semaphore()
    for dim in dims:
        pl.semaphore_signal(barrier, inc=1, device_id=partner(*dim), device_id_type=MESH)
    xbuf[cube_index(dims, set(dims))] = pay_ref[...]
    pl.semaphore_wait(barrier, nb)

    def g_copy(part, step):
        tail = (slice(None), slice(part * full // 2, (part + 1) * full // 2))
        return gather_copy(xbuf, dims, orders[part], step, tail, g_s.at[part, step], g_r.at[part, step])

    for part in range(2):
        g_copy(part, 0).start()
    for step in range(nb):
        for part in range(2):
            g_copy(part, step).wait()
            if step + 1 < nb:
                g_copy(part, step + 1).start()
    for load in loads:
        load.wait()

    expert = lax.axis_index("prompt") * nd + lax.axis_index("decode")
    rest_dims = (2,) * (nb - lead)
    m = 16 * 2 ** (nb - lead)

    def block(i, carry):
        at = tuple((i // (1 << (lead - 1 - k))) % 2 for k in range(lead))
        at = at + (slice(None),) * (nb - lead + 1)
        x = xbuf[at + (slice(0, width),)].reshape(m, width)
        gates = xbuf[at + (slice(width, full),)].reshape(m, full - width).astype(F32)
        both = gates[:, 0 : (full - width) // 2] + gates[:, (full - width) // 2 :]
        lane = lax.broadcasted_iota(jnp.int32, both.shape, 1)
        gate = jnp.sum(jnp.where(lane == expert, both, 0.0), axis=1, keepdims=True)
        gated = jnp.dot(x, wg[...], preferred_element_type=F32)
        lifted = jnp.dot(x, wu[...], preferred_element_type=F32)
        act = (gated / (1.0 + jnp.exp(-gated)) * lifted).astype(BF)
        for c in range(0, width, 1024):
            y = jnp.dot(act, wd[:, c : c + 1024], preferred_element_type=F32)
            y = jnp.where(gate > 0, gate * y, 0.0).astype(BF)
            xbuf[at + (slice(c, c + 1024),)] = y.reshape(rest_dims + (16, 1024))
        return carry

    lax.fori_loop(0, 1 << lead, block, 0)

    half = width // 2

    def p_copy(part, step):
        tail = (slice(None), slice(part * half, (part + 1) * half))
        return scatter_copy(
            xbuf, lands[part][step], dims, orders[part][::-1], step, tail,
            p_s.at[part, step], p_r.at[part, step],
        )

    for part in range(2):
        p_copy(part, 0).start()
    for step in range(nb):
        for part in range(2):
            p_copy(part, step).wait()
            span = slice(part * half, (part + 1) * half)
            at = cube_index(dims, set(orders[part][::-1][: step + 1])) + (slice(None), span)
            summed = xbuf[at].astype(F32) + lands[part][step][...].astype(F32)
            if step + 1 < nb:
                xbuf[at] = summed.astype(BF)
                p_copy(part, step + 1).start()
            else:
                out_ref[:, span] = (res_ref[:, span] + summed).astype(BF)


def per_device(
    np_, nd, hidden_in, queries, new_kv, prompt_kv, sample_kv, counts, out_proj, norm_gain,
    expert_ids, expert_gates, w_gate, w_up, w_down,
):
    prompts, samples, width = hidden_in.shape
    rows = prompts * samples
    hpd = out_proj.shape[0] // HD
    tile = hpd * samples
    groups = H // hpd
    tdt = BF if tile % 16 == 0 else F32
    gen = sample_kv.shape[2]
    experts = np_ * nd
    vmem = pl.BlockSpec(memory_space=pltpu.VMEM)
    hbm = pl.BlockSpec(memory_space=pl.ANY)

    q = queries.reshape(prompts, samples, groups, hpd, HD).transpose(0, 2, 3, 1, 4)
    q = q.reshape(prompts, groups, tile, HD).astype(tdt)
    cols = rows * gen + 128
    col = jnp.arange(cols, dtype=jnp.int32)[None, :]
    row = jnp.arange(rows, dtype=jnp.int32)[:, None]
    own = (col // gen == row) & (col % gen < counts.reshape(rows, 1))
    valid = jnp.where(col < rows * gen, own, col - rows * gen == row)
    bias = jnp.where(valid, 0.0, -1.0).astype(F32).reshape(prompts, 1, samples, cols)
    bias = jnp.broadcast_to(bias, (prompts, hpd, samples, cols)).reshape(prompts, tile, cols)
    hot = expert_ids.reshape(rows, TOPK, 1) == jnp.arange(128, dtype=jnp.int32)
    gates = jnp.sum(jnp.where(hot, expert_gates.reshape(rows, TOPK, 1), 0.0), axis=1)
    high = lax.reduce_precision(gates, 8, 7)
    gates = jnp.concatenate([high, gates - high], axis=1).astype(BF)

    nb = nbits(nd)
    half = width // 2
    cube = (2,) * nb
    dma = pltpu.SemaphoreType.DMA
    lands = [pltpu.VMEM((2,) * (nb - 1 - step) + (16, half), BF) for step in range(nb)]
    residual, payload = pl.pallas_call(
        functools.partial(attention_kernel, nd, hpd, tdt),
        out_shape=(
            jax.ShapeDtypeStruct((rows, width), F32),
            jax.ShapeDtypeStruct((rows, width + 256), BF),
        ),
        in_specs=[vmem, hbm, hbm, vmem, vmem, hbm, vmem, vmem, vmem],
        out_specs=(vmem, vmem),
        scratch_shapes=[
            pltpu.VMEM((2,) + cube + (2, groups, tile, HD), tdt),
            pltpu.VMEM(prompt_kv.shape, BF),
            pltpu.VMEM((rows * gen, sample_kv.shape[3]), BF),
            pltpu.VMEM(out_proj.shape, BF),
            pltpu.VMEM((nd, prompts, nd + 1, tile, HD), tdt),
            pltpu.VMEM((nd, prompts, nd + 1, tile, HD), tdt),
            pltpu.VMEM((nd, 16, HD), F32),
            pltpu.VMEM((nd, 16, HD), F32),
            pltpu.VMEM(cube + (16, width), BF),
        ]
        + lands
        + lands
        + [dma((3,)), dma((2, nb)), dma((2, nb)), dma((nd,)), dma((nd,)), dma((nd,)), dma((nd,)),
           dma((2, nb)), dma((2, nb))],
        compiler_params=pltpu.CompilerParams(
            collective_id=0, has_side_effects=True, vmem_limit_bytes=48 * 2**20
        ),
        name="attention",
    )(
        q, prompt_kv, sample_kv.reshape(rows * gen, sample_kv.shape[3]),
        new_kv.reshape(rows, new_kv.shape[2]), bias, out_proj, hidden_in.reshape(rows, width),
        norm_gain.reshape(1, width), gates,
    )

    nb = nbits(np_) + nbits(nd)
    lands = [pltpu.VMEM((2,) * (nb - 1 - step) + (16, half), BF) for step in range(nb)]
    mixed = pl.pallas_call(
        functools.partial(expert_kernel, np_, nd, max(0, nb - 4)),
        out_shape=jax.ShapeDtypeStruct((rows, width), BF),
        in_specs=[vmem, vmem, hbm, hbm, hbm],
        out_specs=vmem,
        scratch_shapes=[
            pltpu.VMEM((2,) * nb + (16, width + 256), BF),
            pltpu.VMEM(w_gate.shape[1:], BF),
            pltpu.VMEM(w_up.shape[1:], BF),
            pltpu.VMEM(w_down.shape[1:], BF),
        ]
        + lands
        + lands
        + [dma((3,)), dma((2, nb)), dma((2, nb)), dma((2, nb)), dma((2, nb))],
        compiler_params=pltpu.CompilerParams(
            collective_id=1, has_side_effects=True, vmem_limit_bytes=62 * 2**20
        ),
        name="experts",
    )(payload, residual, w_gate[0], w_up[0], w_down[0])
    return mixed.reshape(prompts, samples, width)


def solution(mesh):
    in_specs = (
        P("prompt", "decode", None),
        P("prompt", "decode", None),
        P("prompt", "decode", None),
        P("prompt", "decode", None),
        P("prompt", "decode", None, None),
        P("prompt", "decode"),
        P("decode", None),
        P(),
        P("prompt", "decode", None, None),
        P("prompt", "decode", None, None),
        P(("prompt", "decode"), None, None),
        P(("prompt", "decode"), None, None),
        P(("prompt", "decode"), None, None),
    )
    return jax.shard_map(
        functools.partial(per_device, mesh.shape["prompt"], mesh.shape["decode"]),
        mesh=mesh, in_specs=in_specs, out_specs=P("prompt", "decode", None), check_vma=False,
    )
```

time: 341 us -> 144 us (0.42)
  waiting for transfers between devices: 177 us -> 0 us
  Pallas kernels: 0 us -> 131 us
  blocking collectives: 61.2 us -> 0 us
  matrix products: 33.5 us -> 0 us
  local copies, waits for them, and re-layouts: 42.9 us -> 10.7 us
  between operations: 13.6 us -> 0.09 us
  other arithmetic: 8 us -> 0.93 us
  starting transfers between devices: 3.71 us -> 0 us
    pallas_call x0 -> x2, Pallas kernels: none -> 131 us  [the longest x1 84 us: per_device(): pl.pallas_call(functools.partial(expert_kernel, np_, nd, max(0, nb - 4)),...]
    all_gather x1 -> x0, waiting for transfers between devices: 87.8 us -> none  [per_device(): page_all = lax.all_gather(prompt_kv, 'decode', axis=1, tiled=True)]
    all_to_all x2 -> x0, blocking collectives: 61.2 us -> none  [the longest x1 53.1 us: per_device(): lax.all_to_all(outgoing.reshape(experts, capacity, model_width), ('prompt...]
    all_to_all x1 -> x0, waiting for transfers between devices: 48.6 us -> none  [per_device(): lax.all_to_all(finished.reshape(sources, slots_here, model_width), ('prom...]
    reduce_scatter x1 -> x0, waiting for transfers between devices: 39.4 us -> none  [per_device(): lax.psum_scatter(jnp.dot(attention, out_proj, preferred_element_type=jnp....]
    slice x3 -> x0, local copies, waits for them, and re-layouts: 34.2 us -> none  [the longest x2 22.8 us: split_pages(): keys_part = page_rows[..., :kv_heads * head_width]]
    dot_general x9 -> x0, matrix products: 33.5 us -> none  [the longest x1 10.5 us: expert_ffn(): jnp.dot(hidden_act, down_matrix, preferred_element_type=jnp.float32)]
    unnamed x10 -> x12, local copies, waits for them, and re-layouts: 1.48 us -> 5.77 us
  transfers between devices with their start and end apart: 3 -> 0, of which waited for: 3 -> 0; matrix products, arithmetic and copies ran while one was open for 2% -> 0% of each run, Pallas kernels for 0% -> 0%
where the time goes in v1:
time: 144 us; the launch traced here: 143 us
  Pallas kernels  131 us (91%)
  local copies, waits for them, and re-layouts  10.7 us (7%)
    pallas_call x1, Pallas kernels, per_device(): pl.pallas_call(functools.partial(expert_kernel, np_, nd, max(0, nb - 4)),...  84 us
    pallas_call x1, Pallas kernels, per_device(): pl.pallas_call(functools.partial(attention_kernel, nd, hpd, tdt), out_sha...  47.5 us
    unnamed x12, local copies, waits for them, and re-layouts  5.77 us

profile of v1, /device:TPU:0, one launch (start us, length us, event | category | flops | bytes accessed | tf_op | source)
XLA Modules:
  0.0 143.2 jit_solution(8494854317635450231)
XLA Ops:
  0.0 0.8 copy.18
  0.8 0.8 copy.19
  1.5 0.1 select_reduce_fusion
  1.7 0.7 reshape.143.nkv_ref
  2.4 0.8 select_select_fusion
  3.2 0.9 reshape.145.hid_ref
  4.2 0.1 reshape.144.bias_ref
  4.3 0.0 copy-start
  4.3 1.6 %copy-done = bf16[4,512,512]{2,1,0:T(8,128)(2,1)S(1)} copy-done((bf16[4,512,512]{2,1,0:T(8,128)(2,1)S(1)}, bf16[4,512,512]{2,1,0:T(8,128)(2,1)}, u32[]{:S(2)}) %copy-start) | copy-done | bytes 2097176
  5.9 0.0 copy-start.1
  5.9 1.2 copy-done.1
  7.1 0.0 copy-start.4
  7.1 0.9 copy-done.4
  8.0 0.0 copy-start.5
  8.0 0.7 copy-done.5
  8.8 47.5 %attention.1 = (f32[16,4096]{1,0:T(8,128)S(1)}, bf16[16,4352]{1,0:T(8,128)(2,1)S(1)}) custom-call(bf16[4,8,16,128]{3,2,1,0:T(8,128)(2,1)S(1)} %bitcast.13, bf16[4,512,512]{2,1,0:T(8,128)(2,1)S(1)} %copy-done, bf16[1024,512]{1,0:T(8,128)(2,1)S(1)} %bitcast.12, bf16[16,512]{1,0:T(8,128)(2,1)S(1)} %reshape.143.nkv_ref, f32[4,16,1152]{2,1,0:T(8,128)S(1)} %reshape.144.bias_ref, ...), custom_call_target="tpu_custom_call" | custom-call | tf_op jit(solution)/shard_map/attention/pallas_call | solution.py:392
  56.2 0.0 copy-start.2
  56.2 0.7 copy-done.2
  56.9 0.0 copy-start.3
  56.9 0.6 copy-done.3
  57.6 84.0 %experts.1 = bf16[16,4096]{1,0:T(8,128)(2,1)} custom-call(bf16[16,4352]{1,0:T(8,128)(2,1)} %copy-done.3, f32[16,4096]{1,0:T(8,128)} %copy-done.2, bf16[4096,768]{1,0:T(8,128)(2,1)} %bitcast.15, bf16[4096,768]{1,0:T(8,128)(2,1)} %bitcast.16, bf16[768,4096]{1,0:T(8,128)(2,1)} %bitcast.17), custom_call_target="tpu_custom_call" | custom-call | tf_op jit(solution)/shard_map/experts/pallas_call | solution.py:427
  141.5 1.6 %reshape.147 = bf16[4,4,4096]{2,1,0:T(4,128)(2,1)} reshape(bf16[16,4096]{1,0:T(8,128)(2,1)} %experts.1) | data formatting | bytes 262144 | tf_op jit(solution)/shard_map/reshape | solution.py:446
  (7 shorter events, 0.1 us)
Async XLA Ops:
  4.3 1.6 %copy-start = (bf16[4,512,512]{2,1,0:T(8,128)(2,1)S(1)}, bf16[4,512,512]{2,1,0:T(8,128)(2,1)}, u32[]{:S(2)}) copy-start(bf16[4,512,512]{2,1,0:T(8,128)(2,1)} %kv_ref.1) | copy-start | bytes 6291460
  5.9 1.2 copy-start.1
  7.1 0.9 copy-start.4
  8.0 0.7 copy-start.5
  56.2 0.7 copy-start.2
  56.9 0.6 copy-start.3

commit v2 on v1

--- a/solution.py
+++ b/solution.py
@@ -64,9 +64,9 @@
 
 def attention_kernel(
     nd, hpd, tdt,
-    q_ref, kv_ref, skv_ref, nkv_ref, bias_ref, wo_ref, hid_ref, gain_ref, gates_ref,
+    q_ref, kv_ref, skv_ref, nkv_ref, counts_ref, wo_ref, hid_ref, gain_ref, ids_ref, gates_ref,
     res_ref, pay_ref,
-    qall, kv, skv, wo, obuf, orecv, stat, strecv, acc, *rest,
+    qown, qall, kv, skv, wo, obuf, orecv, stat, strecv, acc, *rest,
 ):
     nb = nbits(nd)
     lands = [rest[:nb], rest[nb : 2 * nb]]
@@ -91,8 +91,13 @@
             barrier, inc=1, device_id={"decode": lax.rem(me + k, nd)}, device_id_type=MESH
         )
     mine = cube_index(dims, set(dims))
+    for p in range(4):
+        row = q_ref[p].astype(F32)
+        for hq in range(H // hpd):
+            heads = [row[:, h * HD : (h + 1) * HD] for h in range(hq * hpd, (hq + 1) * hpd)]
+            qown[p, hq] = jnp.concatenate(heads, axis=0).astype(tdt)
     for part in range(2):
-        qall[(part,) + mine] = q_ref[2 * part : 2 * part + 2]
+        qall[(part,) + mine] = qown[2 * part : 2 * part + 2]
     pl.semaphore_wait(barrier, nd - 1)
 
     def q_copy(part, step):
@@ -104,18 +109,33 @@
         q_copy(part, 0).start()
 
     loads[0].wait()
+    gen = skv.shape[2]
+    cached = 16 * gen
+    fresh = jnp.concatenate([nkv_ref[p].astype(F32) for p in range(4)], axis=0).astype(BF)
+    col = lax.broadcasted_iota(jnp.int32, (tile, cached + 128), 1)
+    sample = lax.rem(lax.broadcasted_iota(jnp.int32, (tile, cached + 128), 0), 4)
+    lane4 = lax.broadcasted_iota(jnp.int32, (tile, 4), 1)
+    own4 = lax.rem(lax.broadcasted_iota(jnp.int32, (tile, 4), 0), 4) == lane4
+    biases = []
+    for p in range(4):
+        count = jnp.sum(
+            jnp.where(own4, counts_ref[p : p + 1, :].astype(F32), 0.0), axis=1, keepdims=True
+        ).astype(jnp.int32)
+        first = (sample + 4 * p) * gen
+        valid = ((col >= first) & (col < first + count)) | (col == cached + 4 * p + sample)
+        biases.append(jnp.where(valid, 0.0, -1.0))
+    bias = jnp.concatenate(biases, axis=0).reshape(4, 1, tile, cached + 128)
     for g in range(KVH):
         ks, vs = slice(g * HD, (g + 1) * HD), slice((KVH + g) * HD, (KVH + g + 1) * HD)
         pad = jnp.zeros((112, HD), BF)
-        keys = jnp.concatenate([skv[:, ks], nkv_ref[:, ks], pad], axis=0)
-        values = jnp.concatenate([skv[:, vs], nkv_ref[:, vs], pad], axis=0)
-        rows = q_ref[:, g * kv_heads_dev : (g + 1) * kv_heads_dev].astype(BF)
+        keys = jnp.concatenate([skv[:, :, :, ks].reshape(cached, HD), fresh[:, ks], pad], axis=0)
+        values = jnp.concatenate([skv[:, :, :, vs].reshape(cached, HD), fresh[:, vs], pad], axis=0)
+        rows = qown[:, g * kv_heads_dev : (g + 1) * kv_heads_dev].astype(BF)
         rows = rows.reshape(4 * kv_heads_dev * tile, HD)
         scores = lax.dot_general(
             rows, keys, (((1,), (1,)), ((), ())), preferred_element_type=F32
         ) * SCALE
         cols = scores.shape[1]
-        bias = bias_ref[...].reshape(4, 1, tile, cols)
         masked = jnp.where(bias < 0, LOW, scores.reshape(4, kv_heads_dev, tile, cols))
         masked = masked.reshape(scores.shape)
         top = jnp.max(masked, axis=1, keepdims=True)
@@ -139,32 +159,25 @@
             if step + 1 < nb:
                 q_copy(part, step + 1).start()
 
-    def peer_copies(j):
-        return (
-            pltpu.make_async_remote_copy(
-                src_ref=obuf.at[j], dst_ref=orecv.at[me], send_sem=o_s.at[j], recv_sem=o_r.at[me],
-                device_id={"decode": j}, device_id_type=MESH),
-            pltpu.make_async_remote_copy(
-                src_ref=stat.at[j], dst_ref=strecv.at[me], send_sem=t_s.at[j], recv_sem=t_r.at[me],
-                device_id={"decode": j}, device_id_type=MESH),
-        )
-
-    def from_peer(j):
-        return (
-            pltpu.make_async_remote_copy(
-                src_ref=obuf.at[j], dst_ref=orecv.at[j], send_sem=o_s.at[j], recv_sem=o_r.at[j],
-                device_id={"decode": j}, device_id_type=MESH),
-            pltpu.make_async_remote_copy(
-                src_ref=stat.at[j], dst_ref=strecv.at[j], send_sem=t_s.at[j], recv_sem=t_r.at[j],
-                device_id={"decode": j}, device_id_type=MESH),
-        )
-
+    def out_copy(j, p, source):
+        return pltpu.make_async_remote_copy(
+            src_ref=obuf.at[j, p], dst_ref=orecv.at[source, p],
+            send_sem=o_s.at[j, p], recv_sem=o_r.at[source, p],
+            device_id={"decode": j}, device_id_type=MESH)
+
+    def stat_copy(j, source):
+        return pltpu.make_async_remote_copy(
+            src_ref=stat.at[j], dst_ref=strecv.at[source],
+            send_sem=t_s.at[j], recv_sem=t_r.at[source],
+            device_id={"decode": j}, device_id_type=MESH)
+
+    peers = [lax.rem(me + k, nd) for k in range(1, nd)]
     loads[1].wait()
     m_rows = nd * kv_heads_dev * tile
-    for g in range(KVH):
-        lane = lax.broadcasted_iota(jnp.int32, (m_rows, HD), 1)
-        st = jnp.zeros((m_rows, HD), F32)
-        for p in range(4):
+    lane = lax.broadcasted_iota(jnp.int32, (m_rows, HD), 1)
+    stats = [jnp.zeros((m_rows, HD), F32) for _ in range(KVH)]
+    for p in range(4):
+        for g in range(KVH):
             keys = kv[p, :, g * HD : (g + 1) * HD]
             values = kv[p, :, (KVH + g) * HD : (KVH + g + 1) * HD]
             q_at = (p // 2,) + (slice(None),) * nb + (p % 2, slice(g * kv_heads_dev, (g + 1) * kv_heads_dev))
@@ -179,29 +192,22 @@
             out = out.astype(tdt).reshape(nd, kv_heads_dev, tile, HD)
             for hq in range(kv_heads_dev):
                 obuf[g * kv_heads_dev + hq, p, 0:nd] = out[:, hq]
-            st = jnp.where(lane == 2 * p, top, jnp.where(lane == 2 * p + 1, total, st))
-        st = st.reshape(nd, kv_heads_dev, tile, HD)
+            stats[g] = jnp.where(lane == 2 * p, top, jnp.where(lane == 2 * p + 1, total, stats[g]))
+        for j in peers:
+            out_copy(j, p, me).start()
+    for g in range(KVH):
+        st = stats[g].reshape(nd, kv_heads_dev, tile, HD)
         for hq in range(kv_heads_dev):
             stat[g * kv_heads_dev + hq, 0:8] = st[:, hq].reshape(nd * tile, HD).T[0:8]
-        for hq in range(kv_heads_dev):
-            j = g * kv_heads_dev + hq
-
-            @pl.when(j != me)
-            def _():
-                for copy in peer_copies(j):
-                    copy.start()
-
-            @pl.when(j == me)
-            def _():
-                orecv[me] = obuf[me]
-                strecv[me] = stat[me]
-
-    for j in range(nd):
-
-        @pl.when(j != me)
-        def _():
-            for copy in from_peer(j):
-                copy.wait()
+    for j in peers:
+        stat_copy(j, me).start()
+    orecv[me] = obuf[me]
+    strecv[me] = stat[me]
+    for j in peers:
+        stat_copy(j, j).wait()
+    for p in range(4):
+        for j in peers:
+            out_copy(j, p, j).wait()
 
     turned = strecv[...].reshape(nd * 16, HD).T
     merged = []
@@ -261,63 +267,86 @@
                 acc[at] = summed.astype(BF)
                 p_copy(part, step + 1).start()
             else:
-                res_ref[:, span] = hid_ref[:, span].astype(F32) + summed
+                hidden = [hid_ref[p, :, span].astype(F32) for p in range(4)]
+                res_ref[:, span] = jnp.concatenate(hidden, axis=0) + summed
     residual = res_ref[...]
     scale = lax.rsqrt(jnp.mean(residual * residual, axis=1, keepdims=True) + 1e-06)
     pay_ref[:, 0:width] = (residual * scale * gain_ref[...]).astype(BF)
-    pay_ref[:, width:] = gates_ref[...]
+    ids, gates = ids_ref[0, 0], gates_ref[0, 0]
+    lane = lax.broadcasted_iota(jnp.int32, (16, HD), 1)
+    table = jnp.zeros((16, HD), F32)
+    for k in range(TOPK):
+        table = jnp.where(lane == ids[:, k : k + 1], gates[:, k : k + 1], table)
+    high = table.astype(BF)
+    pay_ref[:, width : width + HD] = high
+    pay_ref[:, width + HD :] = (table - high.astype(F32)).astype(BF)
 
 
 def expert_kernel(
-    np_, nd, lead, pay_ref, res_ref, wg_ref, wu_ref, wd_ref, out_ref, xbuf, wg, wu, wd, *rest
+    np_, nd, pay_ref, res_ref, wg_ref, wu_ref, wd_ref, out_ref, xbuf, wg, wu, wd, zland, *rest
 ):
-    bp, bd = nbits(np_), nbits(nd)
-    nb = bp + bd
+    nb = nbits(nd)
     lands = [rest[:nb], rest[nb : 2 * nb]]
-    local_sem, g_s, g_r, p_s, p_r = rest[2 * nb :]
-    prompt = [("prompt", k) for k in range(bp - 1, -1, -1)]
-    decode = [("decode", k) for k in range(bd - 1, -1, -1)]
-    dims = prompt + decode
-    orders = [prompt + decode, prompt + decode[:-1][::-1] + decode[-1:]]
+    local_sem, g_s, g_r, r_s, r_r, z_s, z_r, y_s, y_r = rest[2 * nb :]
+    dims = [("decode", k) for k in range(nb - 1, -1, -1)]
+    orders = [dims, dims[:-1][::-1] + dims[-1:]]
+    mine = cube_index(dims, set(dims))
     width = res_ref.shape[1]
     full = pay_ref.shape[1]
+    half = width // 2
+    spans = [slice(0, half), slice(half, width)]
     loads = [
-        pltpu.make_async_copy(wg_ref, wg, local_sem.at[0]),
-        pltpu.make_async_copy(wu_ref, wu, local_sem.at[1]),
-        pltpu.make_async_copy(wd_ref, wd, local_sem.at[2]),
+        pltpu.make_async_copy(wg_ref.at[0], wg, local_sem.at[0]),
+        pltpu.make_async_copy(wu_ref.at[0], wu, local_sem.at[1]),
+        pltpu.make_async_copy(wd_ref.at[0], wd, local_sem.at[2]),
     ]
     for load in loads:
         load.start()
+
+    def across(k):
+        bits = [bit_of("prompt", b) for b in range(nbits(np_))]
+        bits = [1 - bit if (k >> b) % 2 else bit for b, bit in enumerate(bits)]
+        return {"prompt": sum(bit * (1 << b) for b, bit in enumerate(bits))}
+
     barrier = pltpu.get_barrier_semaphore()
     for dim in dims:
         pl.semaphore_signal(barrier, inc=1, device_id=partner(*dim), device_id_type=MESH)
-    xbuf[cube_index(dims, set(dims))] = pay_ref[...]
-    pl.semaphore_wait(barrier, nb)
-
-    def g_copy(part, step):
+    for k in range(1, np_):
+        pl.semaphore_signal(barrier, inc=1, device_id=across(k), device_id_type=MESH)
+    xbuf[(0,) + mine] = pay_ref[...]
+    pl.semaphore_wait(barrier, nb + np_ - 1)
+
+    def z_in(k):
+        return pltpu.make_async_remote_copy(
+            src_ref=pay_ref, dst_ref=xbuf.at[(k,) + mine], send_sem=z_s.at[k], recv_sem=z_r.at[k],
+            device_id=across(k), device_id_type=MESH)
+
+    def z_out(k):
+        return pltpu.make_async_remote_copy(
+            src_ref=xbuf.at[(k,) + mine + (slice(None), slice(0, width))], dst_ref=zland.at[k],
+            send_sem=y_s.at[k], recv_sem=y_r.at[k], device_id=across(k), device_id_type=MESH)
+
+    def gather(k, part, step):
         tail = (slice(None), slice(part * full // 2, (part + 1) * full // 2))
-        return gather_copy(xbuf, dims, orders[part], step, tail, g_s.at[part, step], g_r.at[part, step])
-
-    for part in range(2):
-        g_copy(part, 0).start()
-    for step in range(nb):
-        for part in range(2):
-            g_copy(part, step).wait()
-            if step + 1 < nb:
-                g_copy(part, step + 1).start()
-    for load in loads:
-        load.wait()
+        return gather_copy(
+            xbuf.at[k], dims, orders[part], step, tail, g_s.at[k, part, step], g_r.at[k, part, step]
+        )
+
+    def scatter(k, part, step):
+        return scatter_copy(
+            xbuf.at[k], lands[part][step].at[k], dims, orders[part][::-1], step,
+            (slice(None), spans[part]), r_s.at[k, part, step], r_r.at[k, part, step],
+        )
 
     expert = lax.axis_index("prompt") * nd + lax.axis_index("decode")
-    rest_dims = (2,) * (nb - lead)
-    m = 16 * 2 ** (nb - lead)
-
-    def block(i, carry):
-        at = tuple((i // (1 << (lead - 1 - k))) % 2 for k in range(lead))
-        at = at + (slice(None),) * (nb - lead + 1)
+    m = nd * 16
+    cube = (2,) * nb
+
+    def compute(k):
+        at = (k,) + (slice(None),) * (nb + 1)
         x = xbuf[at + (slice(0, width),)].reshape(m, width)
         gates = xbuf[at + (slice(width, full),)].reshape(m, full - width).astype(F32)
-        both = gates[:, 0 : (full - width) // 2] + gates[:, (full - width) // 2 :]
+        both = gates[:, 0:HD] + gates[:, HD:]
         lane = lax.broadcasted_iota(jnp.int32, both.shape, 1)
         gate = jnp.sum(jnp.where(lane == expert, both, 0.0), axis=1, keepdims=True)
         gated = jnp.dot(x, wg[...], preferred_element_type=F32)
@@ -326,33 +355,53 @@
         for c in range(0, width, 1024):
             y = jnp.dot(act, wd[:, c : c + 1024], preferred_element_type=F32)
             y = jnp.where(gate > 0, gate * y, 0.0).astype(BF)
-            xbuf[at + (slice(c, c + 1024),)] = y.reshape(rest_dims + (16, 1024))
-        return carry
-
-    lax.fori_loop(0, 1 << lead, block, 0)
-
-    half = width // 2
-
-    def p_copy(part, step):
-        tail = (slice(None), slice(part * half, (part + 1) * half))
-        return scatter_copy(
-            xbuf, lands[part][step], dims, orders[part][::-1], step, tail,
-            p_s.at[part, step], p_r.at[part, step],
-        )
-
-    for part in range(2):
-        p_copy(part, 0).start()
-    for step in range(nb):
+            xbuf[at + (slice(c, c + 1024),)] = y.reshape(cube + (16, 1024))
+
+    def reduce(k, step):
         for part in range(2):
-            p_copy(part, step).wait()
-            span = slice(part * half, (part + 1) * half)
-            at = cube_index(dims, set(orders[part][::-1][: step + 1])) + (slice(None), span)
-            summed = xbuf[at].astype(F32) + lands[part][step][...].astype(F32)
-            if step + 1 < nb:
+            scatter(k, part, step - 1).wait()
+            at = (k,) + cube_index(dims, set(orders[part][::-1][:step])) + (slice(None), spans[part])
+            summed = xbuf[at].astype(F32) + lands[part][step - 1][k].astype(F32)
+            if step == nb and k == 0:
+                res_ref_sum = res_ref[:, spans[part]] + summed
+                for other in range(1, np_):
+                    if part == 0:
+                        z_out(other).wait()
+                    res_ref_sum = res_ref_sum + zland[other, :, spans[part]].astype(F32)
+                for p in range(4):
+                    out_ref[p, :, spans[part]] = res_ref_sum[4 * p : 4 * p + 4].astype(BF)
+            else:
                 xbuf[at] = summed.astype(BF)
-                p_copy(part, step + 1).start()
-            else:
-                out_ref[:, span] = (res_ref[:, span] + summed).astype(BF)
+                if step < nb:
+                    scatter(k, part, step).start()
+        if step == nb and k > 0:
+            z_out(k).start()
+
+    for k in range(1, np_):
+        z_in(k).start()
+    for tick in range(1 + 2 * nb + np_):
+        for k in range(np_):
+            step = tick - k
+            if 0 <= step <= nb:
+                if step == 0 and k > 0:
+                    z_in(k).wait()
+                for part in range(2):
+                    if step > 0:
+                        gather(k, part, step - 1).wait()
+                    if step < nb:
+                        gather(k, part, step).start()
+        now = tick - 1 - nb
+        if 0 <= now < np_:
+            if now == 0:
+                for load in loads:
+                    load.wait()
+            compute((now + 1) % np_)
+            for part in range(2):
+                scatter((now + 1) % np_, part, 0).start()
+        for turn in range(np_):
+            step = now - turn
+            if 1 <= step <= nb:
+                reduce((turn + 1) % np_, step)
 
 
 def per_device(
@@ -365,24 +414,8 @@
     tile = hpd * samples
     groups = H // hpd
     tdt = BF if tile % 16 == 0 else F32
-    gen = sample_kv.shape[2]
-    experts = np_ * nd
     vmem = pl.BlockSpec(memory_space=pltpu.VMEM)
     hbm = pl.BlockSpec(memory_space=pl.ANY)
-
-    q = queries.reshape(prompts, samples, groups, hpd, HD).transpose(0, 2, 3, 1, 4)
-    q = q.reshape(prompts, groups, tile, HD).astype(tdt)
-    cols = rows * gen + 128
-    col = jnp.arange(cols, dtype=jnp.int32)[None, :]
-    row = jnp.arange(rows, dtype=jnp.int32)[:, None]
-    own = (col // gen == row) & (col % gen < counts.reshape(rows, 1))
-    valid = jnp.where(col < rows * gen, own, col - rows * gen == row)
-    bias = jnp.where(valid, 0.0, -1.0).astype(F32).reshape(prompts, 1, samples, cols)
-    bias = jnp.broadcast_to(bias, (prompts, hpd, samples, cols)).reshape(prompts, tile, cols)
-    hot = expert_ids.reshape(rows, TOPK, 1) == jnp.arange(128, dtype=jnp.int32)
-    gates = jnp.sum(jnp.where(hot, expert_gates.reshape(rows, TOPK, 1), 0.0), axis=1)
-    high = lax.reduce_precision(gates, 8, 7)
-    gates = jnp.concatenate([high, gates - high], axis=1).astype(BF)
 
     nb = nbits(nd)
     half = width // 2
@@ -395,12 +428,13 @@
             jax.ShapeDtypeStruct((rows, width), F32),
             jax.ShapeDtypeStruct((rows, width + 256), BF),
         ),
-        in_specs=[vmem, hbm, hbm, vmem, vmem, hbm, vmem, vmem, vmem],
+        in_specs=[vmem, hbm, hbm, vmem, vmem, hbm, vmem, vmem, vmem, vmem],
         out_specs=(vmem, vmem),
         scratch_shapes=[
+            pltpu.VMEM((prompts, groups, tile, HD), tdt),
             pltpu.VMEM((2,) + cube + (2, groups, tile, HD), tdt),
             pltpu.VMEM(prompt_kv.shape, BF),
-            pltpu.VMEM((rows * gen, sample_kv.shape[3]), BF),
+            pltpu.VMEM(sample_kv.shape, BF),
             pltpu.VMEM(out_proj.shape, BF),
             pltpu.VMEM((nd, prompts, nd + 1, tile, HD), tdt),
             pltpu.VMEM((nd, prompts, nd + 1, tile, HD), tdt),
@@ -410,40 +444,38 @@
         ]
         + lands
         + lands
-        + [dma((3,)), dma((2, nb)), dma((2, nb)), dma((nd,)), dma((nd,)), dma((nd,)), dma((nd,)),
+        + [dma((3,)), dma((2, nb)), dma((2, nb)), dma((nd, 4)), dma((nd, 4)), dma((nd,)), dma((nd,)),
            dma((2, nb)), dma((2, nb))],
         compiler_params=pltpu.CompilerParams(
             collective_id=0, has_side_effects=True, vmem_limit_bytes=48 * 2**20
         ),
         name="attention",
     )(
-        q, prompt_kv, sample_kv.reshape(rows * gen, sample_kv.shape[3]),
-        new_kv.reshape(rows, new_kv.shape[2]), bias, out_proj, hidden_in.reshape(rows, width),
-        norm_gain.reshape(1, width), gates,
+        queries, prompt_kv, sample_kv, new_kv, counts, out_proj, hidden_in,
+        norm_gain.reshape(1, width), expert_ids, expert_gates,
     )
 
-    nb = nbits(np_) + nbits(nd)
-    lands = [pltpu.VMEM((2,) * (nb - 1 - step) + (16, half), BF) for step in range(nb)]
-    mixed = pl.pallas_call(
-        functools.partial(expert_kernel, np_, nd, max(0, nb - 4)),
-        out_shape=jax.ShapeDtypeStruct((rows, width), BF),
+    lands = [pltpu.VMEM((np_,) + (2,) * (nb - 1 - step) + (16, half), BF) for step in range(nb)]
+    return pl.pallas_call(
+        functools.partial(expert_kernel, np_, nd),
+        out_shape=jax.ShapeDtypeStruct(hidden_in.shape, BF),
         in_specs=[vmem, vmem, hbm, hbm, hbm],
         out_specs=vmem,
         scratch_shapes=[
-            pltpu.VMEM((2,) * nb + (16, width + 256), BF),
+            pltpu.VMEM((np_,) + cube + (16, width + 256), BF),
             pltpu.VMEM(w_gate.shape[1:], BF),
             pltpu.VMEM(w_up.shape[1:], BF),
             pltpu.VMEM(w_down.shape[1:], BF),
+            pltpu.VMEM((np_, rows, width), BF),
         ]
         + lands
         + lands
-        + [dma((3,)), dma((2, nb)), dma((2, nb)), dma((2, nb)), dma((2, nb))],
+        + [dma((3,))] + [dma((np_, 2, nb)) for _ in range(4)] + [dma((np_,)) for _ in range(4)],
         compiler_params=pltpu.CompilerParams(
             collective_id=1, has_side_effects=True, vmem_limit_bytes=62 * 2**20
         ),
         name="experts",
-    )(payload, residual, w_gate[0], w_up[0], w_down[0])
-    return mixed.reshape(prompts, samples, width)
+    )(payload, residual, w_gate, w_up, w_down)
 
 
 def solution(mesh):

time: 144 us -> 118 us (0.82)
  Pallas kernels: 131 us -> 106 us
    pallas_call x1, Pallas kernels: 84 us -> 59.7 us  [per_device(): pl.pallas_call(functools.partial(expert_kernel, np_, nd), out_shape=jax.S...]
    unnamed x12 -> x21, local copies, waits for them, and re-layouts: 5.77 us -> 11.2 us
    reshape x4 -> x0, local copies, waits for them, and re-layouts: 3.39 us -> none  [the longest x1 1.62 us: per_device(): return mixed.reshape(prompts, samples, width)]
where the time goes in v2:
time: 118 us; the launch traced here: 117 us
  Pallas kernels  106 us (90%)
  local copies, waits for them, and re-layouts  11.2 us (9%)
    pallas_call x1, Pallas kernels, per_device(): pl.pallas_call(functools.partial(expert_kernel, np_, nd), out_shape=jax.S...  59.7 us
    pallas_call x1, Pallas kernels, per_device(): pl.pallas_call(functools.partial(attention_kernel, nd, hpd, tdt), out_sha...  46.4 us
    unnamed x21, local copies, waits for them, and re-layouts  11.2 us

profile of v2, /device:TPU:0, one launch (start us, length us, event | category | flops | bytes accessed | tf_op | source)
XLA Modules:
  0.0 117.4 jit_solution(5846771870418343579)
XLA Ops:
  0.0 0.8 copy.14.ids_ref
  0.8 0.8 copy.15.gates_ref
  1.5 0.0 copy-start
  1.5 1.6 %copy-done = bf16[4,512,512]{2,1,0:T(8,128)(2,1)S(1)} copy-done((bf16[4,512,512]{2,1,0:T(8,128)(2,1)S(1)}, bf16[4,512,512]{2,1,0:T(8,128)(2,1)}, u32[]{:S(2)}) %copy-start) | copy-done | bytes 2097176
  3.1 0.0 copy-start.1
  3.1 1.2 %copy-done.1 = bf16[4,4,64,512]{3,2,1,0:T(8,128)(2,1)S(1)} copy-done((bf16[4,4,64,512]{3,2,1,0:T(8,128)(2,1)S(1)}, bf16[4,4,64,512]{3,2,1,0:T(8,128)(2,1)}, u32[]{:S(2)}) %copy-start.1) | copy-done | bytes 1048600
  4.3 0.0 copy-start.4
  4.3 0.9 copy-done.4
  5.2 0.0 copy-start.5
  5.2 0.9 copy-done.5
  6.1 0.0 copy-start.6
  6.1 0.7 copy-done.6
  6.9 0.0 copy-start.7
  6.9 0.7 copy-done.7
  7.6 0.0 copy-start.8
  7.6 0.7 copy-done.8
  8.3 46.4 %attention.1 = (f32[16,4096]{1,0:T(8,128)S(1)}, bf16[16,4352]{1,0:T(8,128)(2,1)S(1)}) custom-call(bf16[4,4,4096]{2,1,0:T(4,128)(2,1)S(1)} %copy-done.4, bf16[4,512,512]{2,1,0:T(8,128)(2,1)S(1)} %copy-done, bf16[4,4,64,512]{3,2,1,0:T(8,128)(2,1)S(1)} %copy-done.1, bf16[4,4,512]{2,1,0:T(4,128)(2,1)S(1)} %copy-done.6, s32[4,4]{1,0:T(4,128)S(1)} %copy-done.8, ...), custom_call_target="tpu_custom_call" | custom-call | tf_op jit(solution)/shard_map/attention/pallas_call | solution.py:425
  54.7 0.0 copy-start.2
  54.7 0.7 copy-done.2
  55.4 0.0 copy-start.3
  55.4 0.7 copy-done.3
  56.1 59.7 %experts.1 = bf16[4,4,4096]{2,1,0:T(4,128)(2,1)} custom-call(bf16[16,4352]{1,0:T(8,128)(2,1)} %copy-done.3, f32[16,4096]{1,0:T(8,128)} %copy-done.2, bf16[1,4096,768]{2,1,0:T(8,128)(2,1)} %wg_ref.1, bf16[1,4096,768]{2,1,0:T(8,128)(2,1)} %wu_ref.1, bf16[1,768,4096]{2,1,0:T(8,128)(2,1)} %wd_ref.1), custom_call_target="tpu_custom_call" | custom-call | tf_op jit(solution)/shard_map/experts/pallas_call | solution.py:459
  115.8 1.6 %copy.17 = bf16[4,4,4096]{2,1,0:T(4,128)(2,1)} copy(bf16[4,4,4096]{2,1,0:T(4,128)(2,1)} %experts.1) | data formatting | bytes 262144
Async XLA Ops:
  1.5 1.6 %copy-start = (bf16[4,512,512]{2,1,0:T(8,128)(2,1)S(1)}, bf16[4,512,512]{2,1,0:T(8,128)(2,1)}, u32[]{:S(2)}) copy-start(bf16[4,512,512]{2,1,0:T(8,128)(2,1)} %kv_ref.1) | copy-start | bytes 6291460
  3.1 1.2 %copy-start.1 = (bf16[4,4,64,512]{3,2,1,0:T(8,128)(2,1)S(1)}, bf16[4,4,64,512]{3,2,1,0:T(8,128)(2,1)}, u32[]{:S(2)}) copy-start(bf16[4,4,64,512]{3,2,1,0:T(8,128)(2,1)} %skv_ref.1) | copy-start | bytes 3145732
  4.3 0.9 copy-start.4
  5.2 0.9 copy-start.5
  6.1 0.7 copy-start.6
  6.9 0.7 copy-start.7
  7.6 0.7 copy-start.8
  54.7 0.7 copy-start.2
  55.4 0.7 copy-start.3

commit v3 on v2

--- a/solution.py
+++ b/solution.py
@@ -64,23 +64,42 @@
 
 def attention_kernel(
     nd, hpd, tdt,
-    q_ref, kv_ref, skv_ref, nkv_ref, counts_ref, wo_ref, hid_ref, gain_ref, ids_ref, gates_ref,
+    q_hbm, kv_ref, skv_ref, nkv_hbm, counts_ref, wo_ref, hid_hbm, gain_ref, ids_ref, gates_ref,
     res_ref, pay_ref,
-    qown, qall, kv, skv, wo, obuf, orecv, stat, strecv, acc, *rest,
+    q_ref, nkv_ref, hid_ref, qown, qall, kv, skv, wo, obuf, orecv, sbuf, srecv,
+    stat, strecv, sstat, ssrecv, acc, *rest,
 ):
     nb = nbits(nd)
     lands = [rest[:nb], rest[nb : 2 * nb]]
-    local_sem, q_s, q_r, o_s, o_r, t_s, t_r, p_s, p_r = rest[2 * nb :]
+    local_sem, q_s, q_r, k_s, k_r, o_s, o_r, t_s, t_r, d_s, d_r, e_s, e_r, p_s, p_r = rest[2 * nb :]
     me = lax.axis_index("decode")
     dims = [("decode", k) for k in range(nb - 1, -1, -1)]
-    orders = [dims[:-1][::-1] + dims[-1:], dims[:-1] + dims[-1:]]
+    orders = [dims[-1:] + dims[:-1][::-1], dims[-1:] + dims[:-1]]
     tile = hpd * 4
-    kv_heads_dev = GROUPS // hpd
+    kvd = GROUPS // hpd
+    g_mine = bit_of("decode", 0)
+    g_mate = 1 - g_mine
+    mate = partner("decode", 0)
+    pair = me // 2
+
+    def kv_part(g, which):
+        at = pl.ds(pl.multiple_of((g + which * KVH) * HD, HD), HD)
+        return kv_ref.at[:, :, at], kv.at[g_mine, :, :, which * HD : (which + 1) * HD]
+
+    def kv_send(which):
+        src, dst = kv_part(g_mate, which)
+        return pltpu.make_async_remote_copy(
+            src_ref=src, dst_ref=dst, send_sem=k_s.at[which], recv_sem=k_r.at[which],
+            device_id=mate, device_id_type=MESH)
 
     loads = [
-        pltpu.make_async_copy(skv_ref, skv, local_sem.at[0]),
-        pltpu.make_async_copy(kv_ref, kv, local_sem.at[1]),
-        pltpu.make_async_copy(wo_ref, wo, local_sem.at[2]),
+        pltpu.make_async_copy(q_hbm, q_ref, local_sem.at[0]),
+        pltpu.make_async_copy(nkv_hbm, nkv_ref, local_sem.at[1]),
+        pltpu.make_async_copy(skv_ref, skv, local_sem.at[2]),
+        pltpu.make_async_copy(*kv_part(g_mine, 0), local_sem.at[3]),
+        pltpu.make_async_copy(*kv_part(g_mine, 1), local_sem.at[4]),
+        pltpu.make_async_copy(wo_ref, wo, local_sem.at[5]),
+        pltpu.make_async_copy(hid_hbm, hid_ref, local_sem.at[6]),
     ]
     for load in loads:
         load.start()
@@ -91,24 +110,36 @@
             barrier, inc=1, device_id={"decode": lax.rem(me + k, nd)}, device_id_type=MESH
         )
     mine = cube_index(dims, set(dims))
+    loads[0].wait()
     for p in range(4):
         row = q_ref[p].astype(F32)
         for hq in range(H // hpd):
             heads = [row[:, h * HD : (h + 1) * HD] for h in range(hq * hpd, (hq + 1) * hpd)]
             qown[p, hq] = jnp.concatenate(heads, axis=0).astype(tdt)
     for part in range(2):
-        qall[(part,) + mine] = qown[2 * part : 2 * part + 2]
+        qall[(part,) + mine] = qown[2 * part : 2 * part + 2, pl.ds(g_mine * kvd, kvd)]
     pl.semaphore_wait(barrier, nd - 1)
 
     def q_copy(part, step):
+        if step == 0:
+            return pltpu.make_async_remote_copy(
+                src_ref=qown.at[2 * part : 2 * part + 2, pl.ds(g_mate * kvd, kvd)],
+                dst_ref=qall.at[(part,) + mine], send_sem=q_s.at[part, 0], recv_sem=q_r.at[part, 0],
+                device_id=mate, device_id_type=MESH)
         return gather_copy(
             qall.at[part], dims, orders[part], step, (), q_s.at[part, step], q_r.at[part, step]
         )
 
     for part in range(2):
         q_copy(part, 0).start()
-
-    loads[0].wait()
+    for which in range(2):
+        kv_send(which).start()
+    for part in range(2):
+        q_copy(part, 0).wait()
+        q_copy(part, 1).start()
+
+    loads[1].wait()
+    loads[2].wait()
     gen = skv.shape[2]
     cached = 16 * gen
     fresh = jnp.concatenate([nkv_ref[p].astype(F32) for p in range(4)], axis=0).astype(BF)
@@ -130,102 +161,150 @@
         pad = jnp.zeros((112, HD), BF)
         keys = jnp.concatenate([skv[:, :, :, ks].reshape(cached, HD), fresh[:, ks], pad], axis=0)
         values = jnp.concatenate([skv[:, :, :, vs].reshape(cached, HD), fresh[:, vs], pad], axis=0)
-        rows = qown[:, g * kv_heads_dev : (g + 1) * kv_heads_dev].astype(BF)
-        rows = rows.reshape(4 * kv_heads_dev * tile, HD)
+        rows = qown[:, g * kvd : (g + 1) * kvd].astype(BF)
+        rows = rows.reshape(4 * kvd * tile, HD)
         scores = lax.dot_general(
             rows, keys, (((1,), (1,)), ((), ())), preferred_element_type=F32
         ) * SCALE
         cols = scores.shape[1]
-        masked = jnp.where(bias < 0, LOW, scores.reshape(4, kv_heads_dev, tile, cols))
+        masked = jnp.where(bias < 0, LOW, scores.reshape(4, kvd, tile, cols))
         masked = masked.reshape(scores.shape)
         top = jnp.max(masked, axis=1, keepdims=True)
         weights = jnp.exp(masked - top)
         total = jnp.sum(weights, axis=1, keepdims=True)
         out = jnp.dot(weights.astype(BF), values, preferred_element_type=F32) / total
-        out = out.astype(tdt).reshape(4, kv_heads_dev, tile, HD)
+        out = out.astype(tdt).reshape(4, kvd, tile, HD)
         lane = lax.broadcasted_iota(jnp.int32, (rows.shape[0], HD), 1)
         st = jnp.where(lane == 0, top, jnp.where(lane == 1, total, 0.0))
-        st = st.reshape(4, kv_heads_dev, tile, HD)
-        for hq in range(kv_heads_dev):
-            j = g * kv_heads_dev + hq
-            obuf[j, :, nd] = out[:, hq]
+        st = st.reshape(4, kvd, tile, HD)
+        for hq in range(kvd):
+            j = g * kvd + hq
+            sbuf[j] = out[:, hq]
             block = st[:, hq].reshape(4 * tile, HD)
             block = jnp.concatenate([block, jnp.zeros((HD - 4 * tile, HD), F32)], axis=0)
-            stat[j, 8:16] = block.T[0:8]
-
-    for step in range(nb):
+            sstat[j] = block.T[0:8]
+
+    def own_copy(j, source):
+        return (
+            pltpu.make_async_remote_copy(
+                src_ref=sbuf.at[j], dst_ref=srecv.at[source], send_sem=d_s.at[j],
+                recv_sem=d_r.at[source], device_id={"decode": j}, device_id_type=MESH),
+            pltpu.make_async_remote_copy(
+                src_ref=sstat.at[j], dst_ref=ssrecv.at[source], send_sem=e_s.at[j],
+                recv_sem=e_r.at[source], device_id={"decode": j}, device_id_type=MESH),
+        )
+
+    for step in range(1, nb):
         for part in range(2):
             q_copy(part, step).wait()
             if step + 1 < nb:
                 q_copy(part, step + 1).start()
-
-    def out_copy(j, p, source):
+    peers = [lax.rem(me + k, nd) for k in range(1, nd)]
+    for j in peers:
+        for copy in own_copy(j, me):
+            copy.start()
+    srecv[me] = sbuf[me]
+    ssrecv[me] = sstat[me]
+
+    g_head = me // kvd
+
+    def out_copy(hq, p, slot):
         return pltpu.make_async_remote_copy(
-            src_ref=obuf.at[j, p], dst_ref=orecv.at[source, p],
-            send_sem=o_s.at[j, p], recv_sem=o_r.at[source, p],
-            device_id={"decode": j}, device_id_type=MESH)
-
-    def stat_copy(j, source):
+            src_ref=obuf.at[hq, p], dst_ref=orecv.at[slot, p],
+            send_sem=o_s.at[hq, p], recv_sem=o_r.at[slot, p],
+            device_id={"decode": g_mine * kvd + hq}, device_id_type=MESH)
+
+    def stat_copy(hq, slot):
         return pltpu.make_async_remote_copy(
-            src_ref=stat.at[j], dst_ref=strecv.at[source],
-            send_sem=t_s.at[j], recv_sem=t_r.at[source],
-            device_id={"decode": j}, device_id_type=MESH)
-
-    peers = [lax.rem(me + k, nd) for k in range(1, nd)]
-    loads[1].wait()
-    m_rows = nd * kv_heads_dev * tile
+            src_ref=stat.at[hq], dst_ref=strecv.at[slot],
+            send_sem=t_s.at[hq], recv_sem=t_r.at[slot],
+            device_id={"decode": g_mine * kvd + hq}, device_id_type=MESH)
+
+    turns = [lax.rem(pair + 1 + k, kvd) for k in range(kvd)]
+    for load in loads[3:5]:
+        load.wait()
+    for which in range(2):
+        kv_send(which).wait()
+    m_rows = nd * kvd * tile
     lane = lax.broadcasted_iota(jnp.int32, (m_rows, HD), 1)
-    stats = [jnp.zeros((m_rows, HD), F32) for _ in range(KVH)]
+    st = jnp.zeros((m_rows, HD), F32)
+    positions = 2 * kv.shape[2]
     for p in range(4):
-        for g in range(KVH):
-            keys = kv[p, :, g * HD : (g + 1) * HD]
-            values = kv[p, :, (KVH + g) * HD : (KVH + g + 1) * HD]
-            q_at = (p // 2,) + (slice(None),) * nb + (p % 2, slice(g * kv_heads_dev, (g + 1) * kv_heads_dev))
-            rows = qall[q_at].astype(BF).reshape(m_rows, HD)
-            scores = lax.dot_general(
-                rows, keys, (((1,), (1,)), ((), ())), preferred_element_type=F32
-            ) * SCALE
-            top = jnp.max(scores, axis=1, keepdims=True)
-            weights = jnp.exp(scores - top)
-            total = jnp.sum(weights, axis=1, keepdims=True)
-            out = jnp.dot(weights.astype(BF), values, preferred_element_type=F32) / total
-            out = out.astype(tdt).reshape(nd, kv_heads_dev, tile, HD)
-            for hq in range(kv_heads_dev):
-                obuf[g * kv_heads_dev + hq, p, 0:nd] = out[:, hq]
-            stats[g] = jnp.where(lane == 2 * p, top, jnp.where(lane == 2 * p + 1, total, stats[g]))
-        for j in peers:
-            out_copy(j, p, me).start()
-    for g in range(KVH):
-        st = stats[g].reshape(nd, kv_heads_dev, tile, HD)
-        for hq in range(kv_heads_dev):
-            stat[g * kv_heads_dev + hq, 0:8] = st[:, hq].reshape(nd * tile, HD).T[0:8]
+        keys = kv[:, p, :, 0:HD].reshape(positions, HD)
+        values = kv[:, p, :, HD : 2 * HD].reshape(positions, HD)
+        rows = qall[(p // 2,) + (slice(None),) * nb + (p % 2,)].astype(BF).reshape(m_rows, HD)
+        scores = lax.dot_general(
+            rows, keys, (((1,), (1,)), ((), ())), preferred_element_type=F32
+        ) * SCALE
+        top = jnp.max(scores, axis=1, keepdims=True)
+        weights = jnp.exp(scores - top)
+        total = jnp.sum(weights, axis=1, keepdims=True)
+        out = jnp.dot(weights.astype(BF), values, preferred_element_type=F32) / total
+        out = out.astype(tdt).reshape(nd, kvd, tile, HD)
+        for hq in range(kvd):
+            obuf[hq, p] = out[:, hq]
+        st = jnp.where(lane == 2 * p, top, jnp.where(lane == 2 * p + 1, total, st))
+        for hq in turns:
+
+            @pl.when(g_mine * kvd + hq != me)
+            def _():
+                out_copy(hq, p, pair).start()
+
+    st = st.reshape(nd, kvd, tile, HD)
+    for hq in range(kvd):
+        stat[hq] = st[:, hq].reshape(nd * tile, HD).T[0:8]
+    for hq in turns:
+
+        @pl.when(g_mine * kvd + hq != me)
+        def _():
+            stat_copy(hq, pair).start()
+
+        @pl.when(g_mine * kvd + hq == me)
+        def _():
+            orecv[pair] = obuf[hq]
+            strecv[pair] = stat[hq]
+
     for j in peers:
-        stat_copy(j, me).start()
-    orecv[me] = obuf[me]
-    strecv[me] = stat[me]
-    for j in peers:
-        stat_copy(j, j).wait()
-    for p in range(4):
-        for j in peers:
-            out_copy(j, p, j).wait()
-
-    turned = strecv[...].reshape(nd * 16, HD).T
+        for copy in own_copy(j, j):
+            copy.wait()
+    for slot in range(nd // 2):
+
+        @pl.when(2 * slot + g_head != me)
+        def _():
+            for p in range(4):
+                out_copy(0, p, slot).wait_recv()
+            stat_copy(0, slot).wait_recv()
+
+    for hq in range(kvd):
+
+        @pl.when(g_mine * kvd + hq != me)
+        def _():
+            for p in range(4):
+                out_copy(hq, p, pair).wait_send()
+            stat_copy(hq, pair).wait_send()
+
+    nc = nd // 2
+    turned = jnp.concatenate(
+        [strecv[...].reshape(nc * 8, HD), ssrecv[...].reshape(nd * 8, HD), jnp.zeros((nd * 4, HD), F32)],
+        axis=0,
+    ).T
     merged = []
     for p in range(4):
-        tops = [turned[:, b * 16 + 2 * p : b * 16 + 2 * p + 1] for b in range(nd)]
-        sums = [turned[:, b * 16 + 2 * p + 1 : b * 16 + 2 * p + 2] for b in range(nd)]
+        tops = [turned[:, b * 8 + 2 * p : b * 8 + 2 * p + 1] for b in range(nc)]
+        sums = [turned[:, b * 8 + 2 * p + 1 : b * 8 + 2 * p + 2] for b in range(nc)]
         span = slice(p * tile, (p + 1) * tile)
-        tops.append(jnp.concatenate([turned[span, d * 16 + 8 : d * 16 + 9] for d in range(nd)], axis=0))
-        sums.append(jnp.concatenate([turned[span, d * 16 + 9 : d * 16 + 10] for d in range(nd)], axis=0))
+        ats = [(nc + d) * 8 for d in range(nd)]
+        tops.append(jnp.concatenate([turned[span, at : at + 1] for at in ats], axis=0))
+        sums.append(jnp.concatenate([turned[span, at + 1 : at + 2] for at in ats], axis=0))
         best = functools.reduce(jnp.maximum, tops)
         whole = jnp.zeros_like(best)
         joined = jnp.zeros((nd * tile, HD), F32)
-        for b in range(nd + 1):
+        for b in range(nc + 1):
             factor = jnp.exp(tops[b] - best) * sums[b]
-            if b < nd:
-                piece = orecv[b, p, 0:nd].reshape(nd * tile, HD)
+            if b < nc:
+                piece = orecv[b, p].reshape(nd * tile, HD)
             else:
-                piece = jnp.concatenate([orecv[d, p, nd] for d in range(nd)], axis=0)
+                piece = jnp.concatenate([srecv[d, p] for d in range(nd)], axis=0)
             whole = whole + factor
             joined = joined + factor * piece.astype(F32)
         merged.append((joined / whole).astype(BF))
@@ -239,7 +318,8 @@
         picked.append(jnp.dot(select, merged, preferred_element_type=F32).astype(BF))
     attention = jnp.concatenate(picked, axis=1)
 
-    loads[2].wait()
+    loads[5].wait()
+    loads[6].wait()
     width = wo.shape[1]
     half = width // 2
     cube = (2,) * nb
@@ -272,8 +352,11 @@
     residual = res_ref[...]
     scale = lax.rsqrt(jnp.mean(residual * residual, axis=1, keepdims=True) + 1e-06)
     pay_ref[:, 0:width] = (residual * scale * gain_ref[...]).astype(BF)
-    ids, gates = ids_ref[0, 0], gates_ref[0, 0]
-    lane = lax.broadcasted_iota(jnp.int32, (16, HD), 1)
+    routes = jnp.concatenate([ids_ref[...].astype(F32), gates_ref[...]], axis=0)
+    routes = jnp.concatenate([routes, jnp.zeros((16, HD - 16), F32)], axis=1)
+    routes = jnp.concatenate([routes, jnp.zeros((HD - 16, HD), F32)], axis=0).T[0:16]
+    ids, gates = routes[:, 0:TOPK], routes[:, TOPK : 2 * TOPK]
+    lane = lax.broadcasted_iota(jnp.int32, (16, HD), 1).astype(F32)
     table = jnp.zeros((16, HD), F32)
     for k in range(TOPK):
         table = jnp.where(lane == ids[:, k : k + 1], gates[:, k : k + 1], table)
@@ -421,6 +504,10 @@
     half = width // 2
     cube = (2,) * nb
     dma = pltpu.SemaphoreType.DMA
+
+    def turn(table):
+        return table.transpose(0, 1, 3, 2).reshape(TOPK, rows)
+
     lands = [pltpu.VMEM((2,) * (nb - 1 - step) + (16, half), BF) for step in range(nb)]
     residual, payload = pl.pallas_call(
         functools.partial(attention_kernel, nd, hpd, tdt),
@@ -428,31 +515,40 @@
             jax.ShapeDtypeStruct((rows, width), F32),
             jax.ShapeDtypeStruct((rows, width + 256), BF),
         ),
-        in_specs=[vmem, hbm, hbm, vmem, vmem, hbm, vmem, vmem, vmem, vmem],
+        in_specs=[hbm, hbm, hbm, hbm, vmem, hbm, hbm, vmem, vmem, vmem],
         out_specs=(vmem, vmem),
         scratch_shapes=[
+            pltpu.VMEM(queries.shape, BF),
+            pltpu.VMEM(new_kv.shape, BF),
+            pltpu.VMEM(hidden_in.shape, BF),
             pltpu.VMEM((prompts, groups, tile, HD), tdt),
-            pltpu.VMEM((2,) + cube + (2, groups, tile, HD), tdt),
-            pltpu.VMEM(prompt_kv.shape, BF),
+            pltpu.VMEM((2,) + cube + (2, groups // 2, tile, HD), tdt),
+            pltpu.VMEM((2, prompts, prompt_kv.shape[1], 2 * HD), BF),
             pltpu.VMEM(sample_kv.shape, BF),
             pltpu.VMEM(out_proj.shape, BF),
-            pltpu.VMEM((nd, prompts, nd + 1, tile, HD), tdt),
-            pltpu.VMEM((nd, prompts, nd + 1, tile, HD), tdt),
-            pltpu.VMEM((nd, 16, HD), F32),
-            pltpu.VMEM((nd, 16, HD), F32),
+            pltpu.VMEM((nd // 2, prompts, nd, tile, HD), tdt),
+            pltpu.VMEM((nd // 2, prompts, nd, tile, HD), tdt),
+            pltpu.VMEM((nd, prompts, tile, HD), tdt),
+            pltpu.VMEM((nd, prompts, tile, HD), tdt),
+            pltpu.VMEM((nd // 2, 8, HD), F32),
+            pltpu.VMEM((nd // 2, 8, HD), F32),
+            pltpu.VMEM((nd, 8, HD), F32),
+            pltpu.VMEM((nd, 8, HD), F32),
             pltpu.VMEM(cube + (16, width), BF),
         ]
         + lands
         + lands
-        + [dma((3,)), dma((2, nb)), dma((2, nb)), dma((nd, 4)), dma((nd, 4)), dma((nd,)), dma((nd,)),
-           dma((2, nb)), dma((2, nb))],
+        + [dma((7,)), dma((2, nb)), dma((2, nb)), dma((2,)), dma((2,))]
+        + [dma((nd // 2, 4)), dma((nd // 2, 4)), dma((nd // 2,)), dma((nd // 2,))]
+        + [dma((nd,)) for _ in range(4)]
+        + [dma((2, nb)), dma((2, nb))],
         compiler_params=pltpu.CompilerParams(
-            collective_id=0, has_side_effects=True, vmem_limit_bytes=48 * 2**20
+            collective_id=0, has_side_effects=True, vmem_limit_bytes=62 * 2**20
         ),
         name="attention",
     )(
         queries, prompt_kv, sample_kv, new_kv, counts, out_proj, hidden_in,
-        norm_gain.reshape(1, width), expert_ids, expert_gates,
+        norm_gain.reshape(1, width), turn(expert_ids), turn(expert_gates),
     )
 
     lands = [pltpu.VMEM((np_,) + (2,) * (nb - 1 - step) + (16, half), BF) for step in range(nb)]

time: 118 us -> 101 us (0.86)
  local copies, waits for them, and re-layouts: 11.2 us -> 1.61 us
  Pallas kernels: 106 us -> 99.2 us
    unnamed x21 -> x1, local copies, waits for them, and re-layouts: 11.2 us -> 1.61 us
    pallas_call x1, Pallas kernels: 46.4 us -> 38.6 us  [per_device(): pl.pallas_call(functools.partial(attention_kernel, nd, hpd, tdt), out_sha...]
where the time goes in v3:
time: 101 us
  Pallas kernels  99.2 us (98%)
  local copies, waits for them, and re-layouts  1.61 us (2%)
    pallas_call x1, Pallas kernels, per_device(): pl.pallas_call(functools.partial(expert_kernel, np_, nd), out_shape=jax.S...  60.5 us
    pallas_call x1, Pallas kernels, per_device(): pl.pallas_call(functools.partial(attention_kernel, nd, hpd, tdt), out_sha...  38.6 us

profile of v3, /device:TPU:0, one launch (start us, length us, event | category | flops | bytes accessed | tf_op | source)
XLA Modules:
  0.0 100.8 jit_solution(7548731962132766191)
XLA Ops:
  0.0 38.6 %attention.1 = (f32[16,4096]{1,0:T(8,128)}, bf16[16,4352]{1,0:T(8,128)(2,1)}) custom-call(bf16[4,4,4096]{2,1,0:T(4,128)(2,1)} %q_hbm.1, bf16[4,512,512]{2,1,0:T(8,128)(2,1)} %kv_ref.1, bf16[4,4,64,512]{3,2,1,0:T(8,128)(2,1)} %skv_ref.1, bf16[4,4,512]{2,1,0:T(4,128)(2,1)} %nkv_hbm.1, s32[4,4]{1,0:T(4,128)} %counts_ref.1, bf16[512,4096]{1,0:T(8,128)(2,1)} %wo_ref.1, ...), custom_call_target="tpu_custom_call" | custom-call | tf_op jit(solution)/shard_map/attention/pallas_call | solution.py:512
  38.6 60.5 %experts.1 = bf16[4,4,4096]{2,1,0:T(4,128)(2,1)} custom-call(bf16[16,4352]{1,0:T(8,128)(2,1)} %get-tuple-element.7.pay_ref, f32[16,4096]{1,0:T(8,128)} %get-tuple-element.8.res_ref, bf16[1,4096,768]{2,1,0:T(8,128)(2,1)} %wg_ref.1, bf16[1,4096,768]{2,1,0:T(8,128)(2,1)} %wu_ref.1, bf16[1,768,4096]{2,1,0:T(8,128)(2,1)} %wd_ref.1), custom_call_target="tpu_custom_call" | custom-call | tf_op jit(solution)/shard_map/experts/pallas_call | solution.py:555
  99.2 1.6 %copy.15 = bf16[4,4,4096]{2,1,0:T(4,128)(2,1)} copy(bf16[4,4,4096]{2,1,0:T(4,128)(2,1)} %experts.1) | data formatting | bytes 262144

commit v4 on v3

--- a/solution.py
+++ b/solution.py
@@ -323,9 +323,6 @@
     width = wo.shape[1]
     half = width // 2
     cube = (2,) * nb
-    for c in range(0, width, 512):
-        part_sum = jnp.dot(attention, wo[:, c : c + 512], preferred_element_type=F32)
-        acc[(slice(None),) * (nb + 1) + (slice(c, c + 512),)] = part_sum.astype(BF).reshape(cube + (16, 512))
     s_orders = [dims[-1:] + dims[:-1][::-1], dims[-1:] + dims[:-1]]
 
     def p_copy(part, step):
@@ -336,6 +333,9 @@
         )
 
     for part in range(2):
+        for c in range(part * half, (part + 1) * half, 512):
+            part_sum = jnp.dot(attention, wo[:, c : c + 512], preferred_element_type=F32)
+            acc[(slice(None),) * (nb + 1) + (slice(c, c + 512),)] = part_sum.astype(BF).reshape(cube + (16, 512))
         p_copy(part, 0).start()
     for step in range(nb):
         for part in range(2):
@@ -366,7 +366,7 @@
 
 
 def expert_kernel(
-    np_, nd, pay_ref, res_ref, wg_ref, wu_ref, wd_ref, out_ref, xbuf, wg, wu, wd, zland, *rest
+    np_, nd, pay_ref, res_ref, wg_ref, wu_ref, wd_ref, out_ref, xbuf, wg, wu, wd, zland, held, *rest
 ):
     nb = nbits(nd)
     lands = [rest[:nb], rest[nb : 2 * nb]]
@@ -425,20 +425,24 @@
     m = nd * 16
     cube = (2,) * nb
 
-    def compute(k):
+    def activate(k):
+        x = xbuf[(k,) + (slice(None),) * (nb + 1) + (slice(0, width),)].reshape(m, width)
+        gated = jnp.dot(x, wg[...], preferred_element_type=F32)
+        lifted = jnp.dot(x, wu[...], preferred_element_type=F32)
+        return (gated / (1.0 + jnp.exp(-gated)) * lifted).astype(BF)
+
+    def project(k, act):
         at = (k,) + (slice(None),) * (nb + 1)
-        x = xbuf[at + (slice(0, width),)].reshape(m, width)
         gates = xbuf[at + (slice(width, full),)].reshape(m, full - width).astype(F32)
         both = gates[:, 0:HD] + gates[:, HD:]
         lane = lax.broadcasted_iota(jnp.int32, both.shape, 1)
         gate = jnp.sum(jnp.where(lane == expert, both, 0.0), axis=1, keepdims=True)
-        gated = jnp.dot(x, wg[...], preferred_element_type=F32)
-        lifted = jnp.dot(x, wu[...], preferred_element_type=F32)
-        act = (gated / (1.0 + jnp.exp(-gated)) * lifted).astype(BF)
-        for c in range(0, width, 1024):
-            y = jnp.dot(act, wd[:, c : c + 1024], preferred_element_type=F32)
-            y = jnp.where(gate > 0, gate * y, 0.0).astype(BF)
-            xbuf[at + (slice(c, c + 1024),)] = y.reshape(cube + (16, 1024))
+        for part in range(2):
+            for c in range(part * half, (part + 1) * half, 1024):
+                y = jnp.dot(act, wd[:, c : c + 1024], preferred_element_type=F32)
+                y = jnp.where(gate > 0, gate * y, 0.0).astype(BF)
+                xbuf[at + (slice(c, c + 1024),)] = y.reshape(cube + (16, 1024))
+            scatter(k, part, 0).start()
 
     def reduce(k, step):
         for part in range(2):
@@ -474,13 +478,15 @@
                     if step < nb:
                         gather(k, part, step).start()
         now = tick - 1 - nb
+        if now == -1:
+            loads[0].wait()
+            loads[1].wait()
+            held[...] = activate(0)
         if 0 <= now < np_:
             if now == 0:
-                for load in loads:
-                    load.wait()
-            compute((now + 1) % np_)
-            for part in range(2):
-                scatter((now + 1) % np_, part, 0).start()
+                loads[2].wait()
+            block = (now + 1) % np_
+            project(block, activate(block) if block else held[...])
         for turn in range(np_):
             step = now - turn
             if 1 <= step <= nb:
@@ -563,6 +569,7 @@
             pltpu.VMEM(w_up.shape[1:], BF),
             pltpu.VMEM(w_down.shape[1:], BF),
             pltpu.VMEM((np_, rows, width), BF),
+            pltpu.VMEM((nd * rows, w_gate.shape[2]), BF),
         ]
         + lands
         + lands

time: 101 us -> 100 us (0.990)
  no operation moved by 1% of the time
where the time goes in v4:
time: 100 us; the launch traced here: 99.9 us
  Pallas kernels  98.3 us (98%)
  local copies, waits for them, and re-layouts  1.61 us (2%)
    pallas_call x1, Pallas kernels, per_device(): pl.pallas_call(functools.partial(expert_kernel, np_, nd), out_shape=jax.S...  60 us
    pallas_call x1, Pallas kernels, per_device(): pl.pallas_call(functools.partial(attention_kernel, nd, hpd, tdt), out_sha...  38.4 us

profile of v4, /device:TPU:0, one launch (start us, length us, event | category | flops | bytes accessed | tf_op | source)
XLA Modules:
  0.0 99.9 jit_solution(9244502489427316429)
XLA Ops:
  0.0 38.4 %attention.1 = (f32[16,4096]{1,0:T(8,128)}, bf16[16,4352]{1,0:T(8,128)(2,1)}) custom-call(bf16[4,4,4096]{2,1,0:T(4,128)(2,1)} %q_hbm.1, bf16[4,512,512]{2,1,0:T(8,128)(2,1)} %kv_ref.1, bf16[4,4,64,512]{3,2,1,0:T(8,128)(2,1)} %skv_ref.1, bf16[4,4,512]{2,1,0:T(4,128)(2,1)} %nkv_hbm.1, s32[4,4]{1,0:T(4,128)} %counts_ref.1, bf16[512,4096]{1,0:T(8,128)(2,1)} %wo_ref.1, ...), custom_call_target="tpu_custom_call" | custom-call | tf_op jit(solution)/shard_map/attention/pallas_call | solution.py:518
  38.4 60.0 %experts.1 = bf16[4,4,4096]{2,1,0:T(4,128)(2,1)} custom-call(bf16[16,4352]{1,0:T(8,128)(2,1)} %get-tuple-element.7.pay_ref, f32[16,4096]{1,0:T(8,128)} %get-tuple-element.8.res_ref, bf16[1,4096,768]{2,1,0:T(8,128)(2,1)} %wg_ref.1, bf16[1,4096,768]{2,1,0:T(8,128)(2,1)} %wu_ref.1, bf16[1,768,4096]{2,1,0:T(8,128)(2,1)} %wd_ref.1), custom_call_target="tpu_custom_call" | custom-call | tf_op jit(solution)/shard_map/experts/pallas_call | solution.py:561
  98.3 1.6 %copy.15 = bf16[4,4,4096]{2,1,0:T(4,128)(2,1)} copy(bf16[4,4,4096]{2,1,0:T(4,128)(2,1)} %experts.1) | data formatting | bytes 262144
